TPU v7x, 256 devices: a whole 4x4x8 slice. The times are simulated.
256 devices in a mesh: inner: 16 (over z, y_hi), outer: 4 (over y_lo, core), heads: 4 (over x).
Axes of the slice: x: 4, y: 4 (y_hi: 2, y_lo: 2; y = y_hi * 2 + y_lo), z: 8, core: 2. Of those that a mesh axis runs over, the one named last changes fastest.
Arguments:
- query_states: bfloat16 [8192, 4096], P(('inner', 'outer'), 'heads'), parts along dimension 1, may hold values from -8 to 8
- key_states: bfloat16 [8192, 512], P(('inner', 'outer'), 'heads'), parts along dimension 1, may hold values from -4 to 4
- value_states: bfloat16 [8192, 512], P(('inner', 'outer'), 'heads'), parts along dimension 1, may hold values from -6 to 6
- output_grad: bfloat16 [8192, 4096], P(('inner', 'outer'), 'heads'), parts along dimension 1, may hold values from -2 to 2
- positions: int32 [8192], P(('inner', 'outer')), may hold values from 0 to 8191, as said below
Outputs:
- query_grad: bfloat16 [8192, 4096], P(('inner', 'outer'), 'heads'), parts along dimension 1
- key_grad: bfloat16 [8192, 512], P(('inner', 'outer'), 'heads'), parts along dimension 1
- value_grad: bfloat16 [8192, 512], P(('inner', 'outer'), 'heads'), parts along dimension 1
There are 4 independent parts, one for each index of `heads`. A program takes and returns all parts, laid end to end along the dimension named above; an argument that names none is the same for every part. Nothing has to cross between parts.
Inputs may be any that keep to these rules, and one draw needn't show every extreme that they name: Over all rows every position occurs once; each aligned block of 64 stored rows holds 64 consecutive positions in increasing order, the blocks in an order drawn from the seed.
All inputs are finite; a program needn't handle non-finite values.
Results may differ from a plain program's by a relative error of at most 0.017.
Values may be sent and summed in bfloat16 or wider, within the bound.
No kernel may reach another device: no remote copies, remote signals or barrier semaphores. Data moves between devices by JAX's collectives and lax.ppermute only.
A program may use at most 128 MiB of HBM per device.

v0:
```python
import functools

import jax
import jax.numpy as jnp
from jax import lax
from jax.experimental import pallas as pl
from jax.experimental.pallas import tpu as pltpu
from jax.sharding import PartitionSpec as P

F32 = jnp.float32
BF16 = jnp.bfloat16
AXES = ("inner", "outer")
HD = 128
HQ = 8
SPAN = 64
TOK = 128
SHARD = TOK + 16
NZ, NY, NC = 8, 4, 2
ROWS = SPAN * HQ
QB = 2 * NY
KB = 2 * NZ * NC
KEYS = KB * SPAN
CH = 512
PER = CH // SPAN
SCALE = HD ** -0.5
SCALE2 = SCALE * 1.4426950408889634
NEG = -1e30
VMEM_LIMIT = 48 * 1024 * 1024
FROM_BELOW = (2, 0, 3, 1)
FROM_ABOVE = (1, 3, 0, 2)
FROM_FAR = (3, 2, 1, 0)


def flat(z, y, c):
    return ((z % NZ) * NY + y % NY) * NC + c


def moves(fn):
    return [
        (flat(z, y, c), flat(*fn(z, y, c)))
        for z in range(NZ)
        for y in range(NY)
        for c in range(NC)
    ]


def send(x, fn):
    return lax.ppermute(x, AXES, moves(fn))


def to_core(z, y, c):
    return z, y, 1 - c


def along_y(d):
    return lambda z, y, c: (z, y + d, c)


def along_y_by_core(z, y, c):
    return (z, y + 1 if c == 0 else y - 1, c)


def along_z(d):
    return lambda z, y, c: (z + d if c == 0 else z - d, y, c)


def dot_nt(a, b):
    return lax.dot_general(a, b, (((1,), (1,)), ((), ())), preferred_element_type=F32)


def dot_nn(a, b):
    return lax.dot_general(a, b, (((1,), (0,)), ((), ())), preferred_element_type=F32)


def key_shards(refs):
    for ref in refs:
        for i in range(ref.shape[0] // SHARD):
            yield ref, i


def sort_keys(meta, refs, ks, vs):
    for s, (ref, i) in enumerate(key_shards(refs)):
        for b in range(2):
            row = i * SHARD + b * SPAN
            dst = pl.ds(pl.multiple_of(meta[2 * s + b] * SPAN, SPAN), SPAN)
            ks[dst, :] = ref[row:row + SPAN, 0:HD]
            vs[dst, :] = ref[row:row + SPAN, HD:2 * HD]


def fill_rows(parts, out):
    for r, (ref, row) in enumerate(parts):
        for b in range(2):
            for h in range(HQ):
                at = ((r * 2 + b) * HQ + h) * SPAN
                out[at:at + SPAN, :] = ref[row + b * SPAN:row + (b + 1) * SPAN, h * HD:(h + 1) * HD]


def lead():
    u = lax.broadcasted_iota(jnp.int32, (SPAN, ROWS), 0)
    t = lax.broadcasted_iota(jnp.int32, (SPAN, ROWS), 1) % SPAN
    return u - t


def masked(meta, scores, diff, first, qid, fill):
    parts = []
    for b in range(scores.shape[0] // SPAN):
        gap = (qid - meta[KB + first + b]) * SPAN
        part = scores[b * SPAN:(b + 1) * SPAN, :]
        parts.append(jnp.where(diff <= gap, part, fill))
    return jnp.concatenate(parts, axis=0)


def walk(meta, qb, step):
    whole = meta[2 * KB + qb]
    halves = meta[2 * KB + QB + qb]
    fulls = meta[2 * KB + 2 * QB + qb]
    lax.fori_loop(0, whole, lambda j, _: step(j * PER, CH, False), 0)
    lax.fori_loop(0, halves, lambda j, _: step(whole * PER, CH // 2, True), 0)
    lax.fori_loop(0, fulls, lambda j, _: step(whole * PER, CH, True), 0)


def query_rows(qb):
    return pl.ds(pl.multiple_of(qb * ROWS, ROWS), ROWS)


def key_rows(first, size):
    return pl.ds(pl.multiple_of(first * SPAN, CH), size)


def forward_kernel(
    meta, own, ka, kb, xa, xb, q0, g0, qa, qb, qc, st,
    ks, vs, vt, qs, gs, gt, past, sc, ex, mx, hi,
):
    sort_keys(meta, (own, ka, kb, xa, xb), ks, vs)
    for j in range(KEYS // HD):
        vt[0:HD, j * HD:(j + 1) * HD] = vs[j * HD:(j + 1) * HD, :].T
    vt[HD:HD + 16, :] = jnp.ones((16, KEYS), BF16)
    fill_rows(((q0, 0), (qa, 0), (qb, 0), (qc, 0)), qs)
    fill_rows(((g0, 0), (qa, SHARD), (qb, SHARD), (qc, SHARD)), gs)
    for j in range(QB):
        gt[j, :, :] = gs[j * ROWS:(j + 1) * ROWS, :].T
    st[0, :, :] = jnp.full((QB, ROWS), NEG, F32)
    st[1, :, :] = jnp.zeros((QB, ROWS), F32)
    st[2, :, :] = jnp.zeros((QB, ROWS), F32)
    sc[...] = jnp.full_like(sc, NEG)
    ex[...] = jnp.zeros_like(ex)
    mx[...] = jnp.full_like(mx, NEG)
    hi[...] = jnp.full_like(hi, NEG)
    for i in range(4):
        past[i] = 0
    diff = lead()

    def finish(qb, first):
        acc = dot_nn(vt[:, key_rows(first, CH)], ex[...])
        total = acc[HD:HD + 1, :]
        dots = jnp.sum(gt[qb].astype(F32) * acc[0:HD, :], axis=0, keepdims=True)
        row = pl.ds(qb, 1)
        peak, old = mx[...], st[0, row, :]
        top = jnp.maximum(peak, old)
        new_w, old_w = jnp.exp2(peak - top), jnp.exp2(old - top)
        st[0, row, :] = top
        st[1, row, :] = st[1, row, :] * old_w + total * new_w
        st[2, row, :] = st[2, row, :] * old_w + dots * new_w

    def weigh():
        peak = jnp.max(hi[...], axis=0, keepdims=True)
        mx[...] = peak
        ex[...] = jnp.exp2(sc[...] - peak).astype(BF16)

    def block(qb, _):
        qid = meta[2 * KB + 3 * QB + qb]

        def step(first, size, mask):
            finish(past[0], past[1])
            weigh()
            s = dot_nt(ks[key_rows(first, size), :], qs[query_rows(qb), :]) * SCALE2
            if mask:
                s = masked(meta, s, diff, first, qid, NEG)
            sc[0:size, :] = s
            if size < CH:
                sc[size:CH, :] = jnp.full((CH - size, ROWS), NEG, F32)
            hi[...] = jnp.max(s.reshape(size // 8, 8, ROWS), axis=0)
            past[0] = past[2]
            past[1] = past[3]
            past[2] = qb
            past[3] = first
            return 0

        walk(meta, qb, step)
        return 0

    lax.fori_loop(0, QB, block, 0)
    finish(past[0], past[1])
    weigh()
    finish(past[2], past[3])


def regroup(x, order):
    return jnp.concatenate([x[2 * i:2 * i + 2, :] for i in order], axis=0)


def backward_kernel(
    meta, own, ka, kb, xa, xb, q0, g0, qa, qb, qc, st0, sta, stb, stc,
    dq, dhere, daway, ks, vs, kt, qs, gs, dk, dv, qacc, lse, dlt,
):
    sort_keys(meta, (own, ka, kb, xa, xb), ks, vs)
    for j in range(KEYS // HD):
        kt[:, j * HD:(j + 1) * HD] = ks[j * HD:(j + 1) * HD, :].T
    fill_rows(((q0, 0), (qa, 0), (qb, 0), (qc, 0)), qs)
    fill_rows(((g0, 0), (qa, SHARD), (qb, SHARD), (qc, SHARD)), gs)
    same = (0, 1, 2, 3)
    sources = ((st0, same), (sta, FROM_BELOW), (stb, FROM_ABOVE), (stc, FROM_FAR))
    peaks = [regroup(s[0], o) for s, o in sources]
    top = functools.reduce(jnp.maximum, peaks)
    shares = [jnp.exp2(p - top) for p in peaks]
    total = sum(w * regroup(s[1], o) for w, (s, o) in zip(shares, sources))
    dots = sum(w * regroup(s[2], o) for w, (s, o) in zip(shares, sources))
    lse[...] = top + jnp.log2(total)
    dlt[...] = dots / total
    for ref in (dk, dv, qacc):
        ref[...] = jnp.zeros_like(ref)
    diff = lead()

    def block(qb, _):
        rows = query_rows(qb)
        q, g = qs[rows, :], gs[rows, :]
        row_lse, row_dlt = lse[pl.ds(qb, 1), :], dlt[pl.ds(qb, 1), :]
        qid = meta[2 * KB + 3 * QB + qb]

        def step(first, size, mask):
            at = key_rows(first, size)
            p = jnp.exp2(dot_nt(ks[at, :], q) * SCALE2 - row_lse)
            if mask:
                p = masked(meta, p, diff, first, qid, 0.0)
            ds = (p * (dot_nt(vs[at, :], g) - row_dlt)).astype(BF16)
            dv[at, :] += dot_nn(p.astype(BF16), g)
            dk[at, :] += dot_nn(ds, q)
            qacc[qb] += dot_nn(kt[:, at], ds)
            return 0

        walk(meta, qb, step)
        return 0

    lax.fori_loop(0, QB, block, 0)
    for i in range(QB):
        done = (qacc[i] * SCALE).T.astype(BF16)
        for h in range(HQ):
            row = (i % 2) * SPAN
            dq[i // 2, row:row + SPAN, h * HD:(h + 1) * HD] = done[h * SPAN:(h + 1) * SPAN, :]
    for s in range(2 * NZ):
        for b in range(2):
            src = pl.ds(pl.multiple_of(meta[2 * s + b] * SPAN, SPAN), SPAN)
            if s == 0:
                ref, i = dhere, 0
            elif s == 1:
                ref, i = daway, 0
            elif s < 9:
                ref, i = dhere, s - 1
            else:
                ref, i = daway, s - 8
            row = i * TOK + b * SPAN
            ref[row:row + SPAN, 0:HD] = (dk[src, :] * SCALE).astype(BF16)
            ref[row:row + SPAN, HD:2 * HD] = dv[src, :].astype(BF16)


def call(body, outs, scratch, flops):
    vmem = pl.BlockSpec(memory_space=pltpu.VMEM)
    smem = pl.BlockSpec(memory_space=pltpu.SMEM)

    def run(meta, *args):
        return pl.pallas_call(
            body,
            out_shape=outs,
            in_specs=[smem] + [vmem] * len(args),
            out_specs=jax.tree.map(lambda _: vmem, outs),
            scratch_shapes=scratch,
            compiler_params=pltpu.CompilerParams(vmem_limit_bytes=VMEM_LIMIT),
            cost_estimate=pl.CostEstimate(
                flops=flops, bytes_accessed=6 * 1024 * 1024, transcendentals=QB * ROWS * KEYS // 2
            ),
        )(meta, *args)

    return run


def shape(*dims, dtype=BF16):
    return jax.ShapeDtypeStruct(dims, dtype)


def fwd_call(meta, *args):
    rows = QB * ROWS
    return call(
        forward_kernel,
        shape(3, QB, ROWS, dtype=F32),
        [
            pltpu.VMEM((KEYS, HD), BF16),
            pltpu.VMEM((KEYS, HD), BF16),
            pltpu.VMEM((HD + 16, KEYS), BF16),
            pltpu.VMEM((rows, HD), BF16),
            pltpu.VMEM((rows, HD), BF16),
            pltpu.VMEM((QB, HD, ROWS), BF16),
            pltpu.SMEM((4,), jnp.int32),
            pltpu.VMEM((CH, ROWS), F32),
            pltpu.VMEM((CH, ROWS), BF16),
            pltpu.VMEM((1, ROWS), F32),
            pltpu.VMEM((8, ROWS), F32),
        ],
        2 * rows * KEYS * HD,
    )(meta, *args)


def bwd_call(meta, *args):
    rows = QB * ROWS
    return call(
        backward_kernel,
        (shape(NY, TOK, HQ * HD), shape(8 * TOK, 2 * HD), shape(8 * TOK, 2 * HD)),
        [
            pltpu.VMEM((KEYS, HD), BF16),
            pltpu.VMEM((KEYS, HD), BF16),
            pltpu.VMEM((HD, KEYS), BF16),
            pltpu.VMEM((rows, HD), BF16),
            pltpu.VMEM((rows, HD), BF16),
            pltpu.VMEM((KEYS, HD), F32),
            pltpu.VMEM((KEYS, HD), F32),
            pltpu.VMEM((QB, HD, ROWS), F32),
            pltpu.VMEM((QB, ROWS), F32),
            pltpu.VMEM((QB, ROWS), F32),
        ],
        5 * rows * KEYS * HD,
    )(meta, *args)


def on_device(query_states, key_states, value_states, output_grad, positions):
    own_ids = (positions[::SPAN] // SPAN).astype(BF16)
    kv = jnp.concatenate(
        [
            jnp.concatenate([key_states, value_states], axis=1),
            jnp.broadcast_to(jnp.repeat(own_ids, HD)[None, :], (16, 2 * HD)),
        ],
        axis=0,
    )
    qg = jnp.concatenate(
        [
            query_states,
            jnp.broadcast_to(jnp.repeat(own_ids, 4 * HD)[None, :], (16, HQ * HD)),
            output_grad,
        ],
        axis=0,
    )
    qg, kv = lax.optimization_barrier((qg, kv))
    qa = send(qg, along_y(1))
    qb = send(qg, along_y(-1))
    pair = jnp.concatenate([kv, send(kv, to_core)], axis=0)
    third = send(pair, along_z(3))
    first = send(pair, along_z(1))
    qa, qb, first, third = lax.optimization_barrier((qa, qb, first, third))
    lower = lax.axis_index("outer") % NC == 0
    qc = send(jnp.where(lower, qa, qb), along_y_by_core)
    kb = send(jnp.concatenate([first, third[:SHARD]], axis=0), along_z(1))
    ka = jnp.concatenate([first, third], axis=0)
    xa = send(ka, to_core)
    kb, qc = lax.optimization_barrier((kb, qc))
    xb = send(kb, to_core)

    def ids_of(x):
        return x.reshape(-1, SHARD, 2 * HD)[:, TOK, ::HD].reshape(-1)

    kid = jnp.concatenate([ids_of(x) for x in (pair, ka, kb, xa, xb)]).astype(jnp.int32)
    qid = jnp.concatenate(
        [own_ids] + [x[TOK, :: 4 * HD] for x in (qa, qb, qc)]
    ).astype(jnp.int32)
    rank = jnp.sum((kid[None, :] < kid[:, None]).astype(jnp.int32), axis=1)
    slots = jnp.arange(KB, dtype=jnp.int32)
    in_order = jnp.sum(jnp.where(rank[None, :] == slots[:, None], kid[None, :], 0), axis=1)
    below = jnp.sum((kid[None, :] < qid[:, None]).astype(jnp.int32), axis=1)
    upto = jnp.sum((kid[None, :] <= qid[:, None]).astype(jnp.int32), axis=1)
    whole = below // PER
    left = upto - whole * PER
    halves = ((left > 0) & (left <= PER // 2)).astype(jnp.int32)
    fulls = (left > PER // 2).astype(jnp.int32)
    meta = jnp.concatenate([rank, in_order, whole, halves, fulls, qid])

    args = (pair, ka, kb, xa, xb, query_states, output_grad, qa, qb, qc)
    st = fwd_call(meta, *args)
    stats = (st, send(st, along_y(1)), send(st, along_y(-1)), send(st, along_y(2)))
    dq, here, away = bwd_call(meta, *args, *stats)

    terms = [dq[0], send(dq[3], along_y(2)), send(dq[1], along_y(-1)), send(dq[2], along_y(1))]
    query_grad = sum(t.astype(F32) for t in terms).astype(BF16)
    both = here.astype(F32) + send(away, to_core).astype(F32)
    out = both[TOK:].astype(BF16)
    back = [
        send(out[2 * TOK:4 * TOK], along_z(-3)),
        send(out[4 * TOK:6 * TOK], along_z(-2)),
        send(out[:2 * TOK], along_z(-1)),
    ]
    back_far = send(out[6 * TOK:], along_z(-4))
    found = sum(t.astype(F32) for t in back)
    cross = send(found[TOK:].astype(BF16), to_core)
    pair_grad = both[:TOK] + back_far.astype(F32) + found[:TOK] + cross.astype(F32)
    return (
        query_grad,
        pair_grad[:, :HD].astype(BF16),
        pair_grad[:, HD:].astype(BF16),
    )


def solution(mesh):
    in_specs = (
        P(("inner", "outer"), "heads"),
        P(("inner", "outer"), "heads"),
        P(("inner", "outer"), "heads"),
        P(("inner", "outer"), "heads"),
        P(("inner", "outer")),
    )
    out_specs = (
        P(("inner", "outer"), "heads"),
        P(("inner", "outer"), "heads"),
        P(("inner", "outer"), "heads"),
    )
    return jax.shard_map(
        on_device, mesh=mesh, in_specs=in_specs, out_specs=out_specs, check_vma=False
    )
```

profile of v0, /device:TPU:1, one launch (start us, length us, event | category | flops | bytes accessed | tf_op | source)
XLA Modules:
  0.0 101.6 jit_solution(14588616223401098940)
XLA Ops:
  0.6 0.7 slice.78
  1.4 0.1 broadcast_bitcast_fusion.1
  1.5 0.1 broadcast_bitcast_fusion
  1.5 0.8 pad_maximum_fusion.2
  2.3 1.1 %pad_maximum_fusion = bf16[272,1024]{1,0:T(8,128)(2,1)S(1)} fusion(bf16[128,1024]{1,0:T(8,128)(2,1)} %g0.3, bf16[16,1024]{1,0:T(8,128)(2,1)S(1)} %broadcast_in_dim.24, bf16[128,1024]{1,0:T(8,128)(2,1)} %q0.3), kind=kLoop, calls=%fused_computation.1 | loop fusion | flops 1671168 | bytes 1114112 | tf_op jit(solution)/shard_map/concatenate | solution.py:342
  3.4 3.6 %collective-permute-start.2 = (bf16[272,1024]{1,0:T(8,128)(2,1)S(1)}, bf16[272,1024]{1,0:T(8,128)(2,1)S(1)}, u32[]{:S(2)}, u32[]{:S(2)}) collective-permute-start(bf16[272,1024]{1,0:T(8,128)(2,1)S(1)} %pad_maximum_fusion), channel_id=1, source_target_pairs={{0,24},{4,28},{8,0},{12,4},{16,8},{20,12},{24,16},{28,20},{32,56},... | collective-permute-start | bytes 1671176 | tf_op jit(solution)/shard_map/ppermute | solution.py:48
  7.1 1.7 %collective-permute-start = (bf16[144,256]{1,0:T(8,128)(2,1)S(1)}, bf16[144,256]{1,0:T(8,128)(2,1)S(1)}, u32[]{:S(2)}, u32[]{:S(2)}) collective-permute-start(bf16[144,256]{1,0:T(8,128)(2,1)S(1)} %pad_maximum_fusion.2), channel_id=1, source_target_pairs={{0,4},{4,0},{8,12},{12,8},{16,20},{20,16},{24,28},{28,24},{32,36},... | collective-permute-start | bytes 221192 | tf_op jit(solution)/shard_map/ppermute | solution.py:48
  8.8 0.9 collective-permute-done
  9.7 5.7 %collective-permute-start.4 = (bf16[288,256]{1,0:T(8,128)(2,1)S(1)}, bf16[288,256]{1,0:T(8,128)(2,1)S(1)}, u32[]{:S(2)}, u32[]{:S(2)}) collective-permute-start(bf16[288,256]{1,0:T(8,128)(2,1)S(1)} %constant_dynamic-update-slice_fusion.own), channel_id=1, source_target_pairs={{0,96},{4,164},{8,104},{12,172},{16,112},{20,180},{24,120},{28,188... | collective-permute-start | bytes 442376 | tf_op jit(solution)/shard_map/ppermute | solution.py:48
  15.4 0.7 collective-permute-start.3
  16.1 4.5 %collective-permute-done.4 = bf16[288,256]{1,0:T(8,128)(2,1)S(1)} collective-permute-done((bf16[288,256]{1,0:T(8,128)(2,1)S(1)}, bf16[288,256]{1,0:T(8,128)(2,1)S(1)}, u32[]{:S(2)}, u32[]{:S(2)}) %collective-permute-start.4) | collective-permute-done | bytes 147488 | tf_op jit(solution)/shard_map/ppermute | solution.py:48
  20.7 1.6 %collective-permute-done.3 = bf16[288,256]{1,0:T(8,128)(2,1)S(1)} collective-permute-done((bf16[288,256]{1,0:T(8,128)(2,1)S(1)}, bf16[288,256]{1,0:T(8,128)(2,1)S(1)}, u32[]{:S(2)}, u32[]{:S(2)}) %collective-permute-start.3) | collective-permute-done | bytes 147488 | tf_op jit(solution)/shard_map/ppermute | solution.py:48
  22.2 0.1 broadcast_select_fusion
  22.3 0.0 copy-start
  22.3 0.0 copy-start.1
  22.3 3.0 %collective-permute-start.6 = (bf16[272,1024]{1,0:T(8,128)(2,1)S(1)}, bf16[272,1024]{1,0:T(8,128)(2,1)S(1)}, u32[]{:S(2)}, u32[]{:S(2)}) collective-permute-start(bf16[272,1024]{1,0:T(8,128)(2,1)S(1)} %broadcast_select_fusion), channel_id=1, source_target_pairs={{0,8},{4,28},{8,16},{12,4},{16,24},{20,12},{24,0},{28,20},{32,40},... | collective-permute-start | bytes 1671176 | tf_op jit(solution)/shard_map/ppermute | solution.py:48
  25.4 3.4 %collective-permute-start.5 = (bf16[432,256]{1,0:T(8,128)(2,1)S(1)}, bf16[432,256]{1,0:T(8,128)(2,1)S(1)}, u32[]{:S(2)}, u32[]{:S(2)}) collective-permute-start(bf16[432,256]{1,0:T(8,128)(2,1)S(1)} %pad_maximum_fusion.1), channel_id=1, source_target_pairs={{0,32},{4,228},{8,40},{12,236},{16,48},{20,244},{24,56},{28,252},{... | collective-permute-start | bytes 663560 | tf_op jit(solution)/shard_map/ppermute | solution.py:48
  28.8 0.1 collective-permute-start.7
  28.9 2.7 %collective-permute-done.5.kb = bf16[432,256]{1,0:T(8,128)(2,1)S(1)} collective-permute-done((bf16[432,256]{1,0:T(8,128)(2,1)S(1)}, bf16[432,256]{1,0:T(8,128)(2,1)S(1)}, u32[]{:S(2)}, u32[]{:S(2)}) %collective-permute-start.5) | collective-permute-done | bytes 221216 | tf_op jit(solution)/shard_map/ppermute | solution.py:48
  31.6 0.2 collective-permute-done.6.qc
  31.8 2.4 %collective-permute-start.8 = (bf16[432,256]{1,0:T(8,128)(2,1)S(1)}, bf16[432,256]{1,0:T(8,128)(2,1)S(1)}, u32[]{:S(2)}, u32[]{:S(2)}) collective-permute-start(bf16[432,256]{1,0:T(8,128)(2,1)S(1)} %collective-permute-done.5.kb), channel_id=1, source_target_pairs={{0,4},{4,0},{8,12},{12,8},{16,20},{20,16},{24,28},{28,24},{32,36},... | collective-permute-start | bytes 663560 | tf_op jit(solution)/shard_map/ppermute | solution.py:48
  34.2 0.1 slice.79
  34.3 0.1 concatenate.59
  34.4 0.1 slice.85
  34.5 0.1 slice.86
  34.6 0.1 slice.80
  34.7 0.1 concatenate.61
  34.8 0.1 slice.83
  34.9 0.1 concatenate.64
  35.0 0.1 slice.87
  35.1 0.1 slice.82
  35.2 0.1 concatenate.63
  35.3 0.1 maximum_convert_fusion
  35.4 0.1 slice.84
  35.5 0.1 concatenate.65
  35.6 0.1 concatenate.66
  35.7 0.2 convert_reduce_fusion
  35.9 0.1 select_reduce_fusion
  36.0 0.2 convert_reduce_fusion.1
  36.3 0.1 concatenate.71.meta
  36.3 9.6 %shard_map.76.st0 = f32[3,8,512]{2,1,0:T(8,128)S(1)} custom-call(s32[96]{0:T(128)S(1)} %concatenate.71.meta, bf16[288,256]{1,0:T(8,128)(2,1)S(1)} %constant_dynamic-update-slice_fusion.own, bf16[576,256]{1,0:T(8,128)(2,1)S(1)} %constant_dynamic-update-slice_fusion.2.ka, bf16[432,256]{1,0:T(8,128)(2,1)S(1)} %collective-permute-done.5.kb, ...), custom_call_target="tpu_custom_call" | custom-call | flops 2147483648 | bytes 6291456 | tf_op jit(solution)/shard_map/pallas_call | solution.py:271
  46.0 0.1 collective-permute-start.11
  46.1 1.8 %collective-permute-start.10 = (f32[3,8,512]{2,1,0:T(8,128)S(1)}, f32[3,8,512]{2,1,0:T(8,128)S(1)}, u32[]{:S(2)}, u32[]{:S(2)}) collective-permute-start(f32[3,8,512]{2,1,0:T(8,128)S(1)} %shard_map.76.st0), channel_id=1, source_target_pairs={{0,24},{4,28},{8,0},{12,4},{16,8},{20,12},{24,16},{28,20},{32,56},... | collective-permute-start | bytes 147464 | tf_op jit(solution)/shard_map/ppermute | solution.py:48
  47.9 0.5 collective-permute-start.9
  48.4 2.2 %collective-permute-done.11.stc = f32[3,8,512]{2,1,0:T(8,128)S(1)} collective-permute-done((f32[3,8,512]{2,1,0:T(8,128)S(1)}, f32[3,8,512]{2,1,0:T(8,128)S(1)}, u32[]{:S(2)}, u32[]{:S(2)}) %collective-permute-start.11) | collective-permute-done | bytes 49184 | tf_op jit(solution)/shard_map/ppermute | solution.py:48
  50.6 0.0 collective-permute-done.10.stb
  50.6 1.4 %collective-permute-done.9.sta = f32[3,8,512]{2,1,0:T(8,128)S(1)} collective-permute-done((f32[3,8,512]{2,1,0:T(8,128)S(1)}, f32[3,8,512]{2,1,0:T(8,128)S(1)}, u32[]{:S(2)}, u32[]{:S(2)}) %collective-permute-start.9) | collective-permute-done | bytes 49184 | tf_op jit(solution)/shard_map/ppermute | solution.py:48
  52.0 17.0 %shard_map.77 = (bf16[4,128,1024]{2,1,0:T(8,128)(2,1)S(1)}, bf16[1024,256]{1,0:T(8,128)(2,1)S(1)}, bf16[1024,256]{1,0:T(8,128)(2,1)S(1)}) custom-call(s32[96]{0:T(128)S(1)} %concatenate.71.meta, bf16[288,256]{1,0:T(8,128)(2,1)S(1)} %constant_dynamic-update-slice_fusion.own, bf16[576,256]{1,0:T(8,128)(2,1)S(1)} %constant_dynamic-update-slice_fusion.2.ka, ...), custom_call_target="tpu_custom_call" | custom-call | flops 5368709120 | bytes 6291456 | tf_op jit(solution)/shard_map/pallas_call | solution.py:271
  69.0 0.1 collective-permute-start.15
  69.1 1.9 %collective-permute-done.15 = bf16[1024,256]{1,0:T(8,128)(2,1)S(1)} collective-permute-done((bf16[1024,256]{1,0:T(8,128)(2,1)S(1)}, bf16[1024,256]{1,0:T(8,128)(2,1)S(1)}, u32[]{:S(2)}, u32[]{:S(2)}) %collective-permute-start.15) | collective-permute-done | bytes 524320 | tf_op jit(solution)/shard_map/ppermute | solution.py:48
  71.0 0.2 convert_add_fusion
  71.2 9.2 %collective-permute-start.17 = (bf16[256,256]{1,0:T(8,128)(2,1)S(1)}, bf16[256,256]{1,0:T(8,128)(2,1)S(1)}, u32[]{:S(2)}, u32[]{:S(2)}) collective-permute-start(bf16[256,256]{1,0:T(8,128)(2,1)S(1)} %get-tuple-element.34), channel_id=1, source_target_pairs={{0,160},{4,100},{8,168},{12,108},{16,176},{20,116},{24,184},{28,12... | collective-permute-start | bytes 393224 | tf_op jit(solution)/shard_map/ppermute | solution.py:48
  80.5 1.4 %collective-permute-start.19 = (bf16[256,256]{1,0:T(8,128)(2,1)S(1)}, bf16[256,256]{1,0:T(8,128)(2,1)S(1)}, u32[]{:S(2)}, u32[]{:S(2)}) collective-permute-start(bf16[256,256]{1,0:T(8,128)(2,1)S(1)} %get-tuple-element.35), channel_id=1, source_target_pairs={{0,224},{4,36},{8,232},{12,44},{16,240},{20,52},{24,248},{28,60},{... | collective-permute-start | bytes 393224 | tf_op jit(solution)/shard_map/ppermute | solution.py:48
  81.9 2.8 %collective-permute-start.18 = (bf16[256,256]{1,0:T(8,128)(2,1)S(1)}, bf16[256,256]{1,0:T(8,128)(2,1)S(1)}, u32[]{:S(2)}, u32[]{:S(2)}) collective-permute-start(bf16[256,256]{1,0:T(8,128)(2,1)S(1)} %get-tuple-element.36), channel_id=1, source_target_pairs={{0,192},{4,68},{8,200},{12,76},{16,208},{20,84},{24,216},{28,92},{... | collective-permute-start | bytes 393224 | tf_op jit(solution)/shard_map/ppermute | solution.py:48
  84.7 0.1 slice_bitcast_fusion.2
  84.7 0.3 collective-permute-start.12
  85.0 1.7 %collective-permute-start.14 = (bf16[128,1024]{1,0:T(8,128)(2,1)S(1)}, bf16[128,1024]{1,0:T(8,128)(2,1)S(1)}, u32[]{:S(2)}, u32[]{:S(2)}) collective-permute-start(bf16[128,1024]{1,0:T(8,128)(2,1)S(1)} %get-tuple-element.32), channel_id=1, source_target_pairs={{0,8},{4,12},{8,16},{12,20},{16,24},{20,28},{24,0},{28,4},{32,40},... | collective-permute-start | bytes 786440 | tf_op jit(solution)/shard_map/ppermute | solution.py:48
  86.8 1.0 collective-permute-start.13
  87.7 5.7 %collective-permute-start.16 = (bf16[128,256]{1,0:T(8,128)(2,1)S(1)}, bf16[128,256]{1,0:T(8,128)(2,1)S(1)}, u32[]{:S(2)}, u32[]{:S(2)}) collective-permute-start(bf16[128,256]{1,0:T(8,128)(2,1)S(1)} %slice.102), channel_id=1, source_target_pairs={{0,128},{4,132},{8,136},{12,140},{16,144},{20,148},{24,152},{28,15... | collective-permute-start | bytes 196616 | tf_op jit(solution)/shard_map/ppermute | solution.py:48
  93.5 0.1 collective-permute-start.20
  93.6 0.1 collective-permute-done.12
  93.7 6.3 %collective-permute-done.14 = bf16[128,1024]{1,0:T(8,128)(2,1)S(1)} collective-permute-done((bf16[128,1024]{1,0:T(8,128)(2,1)S(1)}, bf16[128,1024]{1,0:T(8,128)(2,1)S(1)}, u32[]{:S(2)}, u32[]{:S(2)}) %collective-permute-start.14) | collective-permute-done | bytes 262176 | tf_op jit(solution)/shard_map/ppermute | solution.py:48
  100.0 0.9 fusion.2
  100.9 0.6 fusion.8
  (36 shorter events, 0.4 us)
Async XLA Ops:
  3.4 18.8 %collective-permute-start.2 = (bf16[272,1024]{1,0:T(8,128)(2,1)S(1)}, bf16[272,1024]{1,0:T(8,128)(2,1)S(1)}, u32[]{:S(2)}, u32[]{:S(2)}) collective-permute-start(bf16[272,1024]{1,0:T(8,128)(2,1)S(1)} %pad_maximum_fusion), channel_id=1, source_target_pairs={{0,24},{4,28},{8,0},{12,4},{16,8},{20,12},{24,16},{28,20},{32,56},... | collective-permute-start | bytes 1671176 | tf_op jit(solution)/shard_map/ppermute | solution.py:48
  7.1 15.2 %collective-permute-start.1 = (bf16[272,1024]{1,0:T(8,128)(2,1)S(1)}, bf16[272,1024]{1,0:T(8,128)(2,1)S(1)}, u32[]{:S(2)}, u32[]{:S(2)}) collective-permute-start(bf16[272,1024]{1,0:T(8,128)(2,1)S(1)} %pad_maximum_fusion), channel_id=1, source_target_pairs={{0,8},{4,12},{8,16},{12,20},{16,24},{20,28},{24,0},{28,4},{32,40},... | collective-permute-start | bytes 1671176 | tf_op jit(solution)/shard_map/ppermute | solution.py:48
  7.1 2.6 %collective-permute-start = (bf16[144,256]{1,0:T(8,128)(2,1)S(1)}, bf16[144,256]{1,0:T(8,128)(2,1)S(1)}, u32[]{:S(2)}, u32[]{:S(2)}) collective-permute-start(bf16[144,256]{1,0:T(8,128)(2,1)S(1)} %pad_maximum_fusion.2), channel_id=1, source_target_pairs={{0,4},{4,0},{8,12},{12,8},{16,20},{20,16},{24,28},{28,24},{32,36},... | collective-permute-start | bytes 221192 | tf_op jit(solution)/shard_map/ppermute | solution.py:48
  9.7 11.0 %collective-permute-start.4 = (bf16[288,256]{1,0:T(8,128)(2,1)S(1)}, bf16[288,256]{1,0:T(8,128)(2,1)S(1)}, u32[]{:S(2)}, u32[]{:S(2)}) collective-permute-start(bf16[288,256]{1,0:T(8,128)(2,1)S(1)} %constant_dynamic-update-slice_fusion.own), channel_id=1, source_target_pairs={{0,96},{4,164},{8,104},{12,172},{16,112},{20,180},{24,120},{28,188... | collective-permute-start | bytes 442376 | tf_op jit(solution)/shard_map/ppermute | solution.py:48
  15.4 6.8 %collective-permute-start.3 = (bf16[288,256]{1,0:T(8,128)(2,1)S(1)}, bf16[288,256]{1,0:T(8,128)(2,1)S(1)}, u32[]{:S(2)}, u32[]{:S(2)}) collective-permute-start(bf16[288,256]{1,0:T(8,128)(2,1)S(1)} %constant_dynamic-update-slice_fusion.own), channel_id=1, source_target_pairs={{0,32},{4,228},{8,40},{12,236},{16,48},{20,244},{24,56},{28,252},{... | collective-permute-start | bytes 442376 | tf_op jit(solution)/shard_map/ppermute | solution.py:48
  22.3 14.0 %copy-start = (bf16[128,1024]{1,0:T(8,128)(2,1)S(1)}, bf16[128,1024]{1,0:T(8,128)(2,1)}, u32[]{:S(2)}) copy-start(bf16[128,1024]{1,0:T(8,128)(2,1)} %g0.3) | copy-start | bytes 786436
  22.3 14.0 %copy-start.1 = (bf16[128,1024]{1,0:T(8,128)(2,1)S(1)}, bf16[128,1024]{1,0:T(8,128)(2,1)}, u32[]{:S(2)}) copy-start(bf16[128,1024]{1,0:T(8,128)(2,1)} %q0.3) | copy-start | bytes 786436
  22.3 9.5 %collective-permute-start.6 = (bf16[272,1024]{1,0:T(8,128)(2,1)S(1)}, bf16[272,1024]{1,0:T(8,128)(2,1)S(1)}, u32[]{:S(2)}, u32[]{:S(2)}) collective-permute-start(bf16[272,1024]{1,0:T(8,128)(2,1)S(1)} %broadcast_select_fusion), channel_id=1, source_target_pairs={{0,8},{4,28},{8,16},{12,4},{16,24},{20,12},{24,0},{28,20},{32,40},... | collective-permute-start | bytes 1671176 | tf_op jit(solution)/shard_map/ppermute | solution.py:48
  25.4 6.3 %collective-permute-start.5 = (bf16[432,256]{1,0:T(8,128)(2,1)S(1)}, bf16[432,256]{1,0:T(8,128)(2,1)S(1)}, u32[]{:S(2)}, u32[]{:S(2)}) collective-permute-start(bf16[432,256]{1,0:T(8,128)(2,1)S(1)} %pad_maximum_fusion.1), channel_id=1, source_target_pairs={{0,32},{4,228},{8,40},{12,236},{16,48},{20,244},{24,56},{28,252},{... | collective-permute-start | bytes 663560 | tf_op jit(solution)/shard_map/ppermute | solution.py:48
  28.8 6.0 %collective-permute-start.7 = (bf16[576,256]{1,0:T(8,128)(2,1)S(1)}, bf16[576,256]{1,0:T(8,128)(2,1)S(1)}, u32[]{:S(2)}, u32[]{:S(2)}) collective-permute-start(bf16[576,256]{1,0:T(8,128)(2,1)S(1)} %constant_dynamic-update-slice_fusion.2.ka), channel_id=1, source_target_pairs={{0,4},{4,0},{8,12},{12,8},{16,20},{20,16},{24,28},{28,24},{32,36},... | collective-permute-start | bytes 884744 | tf_op jit(solution)/shard_map/ppermute | solution.py:48
  31.8 3.6 %collective-permute-start.8 = (bf16[432,256]{1,0:T(8,128)(2,1)S(1)}, bf16[432,256]{1,0:T(8,128)(2,1)S(1)}, u32[]{:S(2)}, u32[]{:S(2)}) collective-permute-start(bf16[432,256]{1,0:T(8,128)(2,1)S(1)} %collective-permute-done.5.kb), channel_id=1, source_target_pairs={{0,4},{4,0},{8,12},{12,8},{16,20},{20,16},{24,28},{28,24},{32,36},... | collective-permute-start | bytes 663560 | tf_op jit(solution)/shard_map/ppermute | solution.py:48
  46.0 4.6 %collective-permute-start.11 = (f32[3,8,512]{2,1,0:T(8,128)S(1)}, f32[3,8,512]{2,1,0:T(8,128)S(1)}, u32[]{:S(2)}, u32[]{:S(2)}) collective-permute-start(f32[3,8,512]{2,1,0:T(8,128)S(1)} %shard_map.76.st0), channel_id=1, source_target_pairs={{0,16},{4,20},{8,24},{12,28},{16,0},{20,4},{24,8},{28,12},{32,48},... | collective-permute-start | bytes 147464 | tf_op jit(solution)/shard_map/ppermute | solution.py:48
  46.1 4.5 %collective-permute-start.10 = (f32[3,8,512]{2,1,0:T(8,128)S(1)}, f32[3,8,512]{2,1,0:T(8,128)S(1)}, u32[]{:S(2)}, u32[]{:S(2)}) collective-permute-start(f32[3,8,512]{2,1,0:T(8,128)S(1)} %shard_map.76.st0), channel_id=1, source_target_pairs={{0,24},{4,28},{8,0},{12,4},{16,8},{20,12},{24,16},{28,20},{32,56},... | collective-permute-start | bytes 147464 | tf_op jit(solution)/shard_map/ppermute | solution.py:48
  47.9 4.2 %collective-permute-start.9 = (f32[3,8,512]{2,1,0:T(8,128)S(1)}, f32[3,8,512]{2,1,0:T(8,128)S(1)}, u32[]{:S(2)}, u32[]{:S(2)}) collective-permute-start(f32[3,8,512]{2,1,0:T(8,128)S(1)} %shard_map.76.st0), channel_id=1, source_target_pairs={{0,8},{4,12},{8,16},{12,20},{16,24},{20,28},{24,0},{28,4},{32,40},... | collective-permute-start | bytes 147464 | tf_op jit(solution)/shard_map/ppermute | solution.py:48
  69.0 2.0 %collective-permute-start.15 = (bf16[1024,256]{1,0:T(8,128)(2,1)S(1)}, bf16[1024,256]{1,0:T(8,128)(2,1)S(1)}, u32[]{:S(2)}, u32[]{:S(2)}) collective-permute-start(bf16[1024,256]{1,0:T(8,128)(2,1)S(1)} %get-tuple-element.24), channel_id=1, source_target_pairs={{0,4},{4,0},{8,12},{12,8},{16,20},{20,16},{24,28},{28,24},{32,36},... | collective-permute-start | bytes 1572872 | tf_op jit(solution)/shard_map/ppermute | solution.py:48
  71.2 15.5 %collective-permute-start.17 = (bf16[256,256]{1,0:T(8,128)(2,1)S(1)}, bf16[256,256]{1,0:T(8,128)(2,1)S(1)}, u32[]{:S(2)}, u32[]{:S(2)}) collective-permute-start(bf16[256,256]{1,0:T(8,128)(2,1)S(1)} %get-tuple-element.34), channel_id=1, source_target_pairs={{0,160},{4,100},{8,168},{12,108},{16,176},{20,116},{24,184},{28,12... | collective-permute-start | bytes 393224 | tf_op jit(solution)/shard_map/ppermute | solution.py:48
  80.5 7.3 %collective-permute-start.19 = (bf16[256,256]{1,0:T(8,128)(2,1)S(1)}, bf16[256,256]{1,0:T(8,128)(2,1)S(1)}, u32[]{:S(2)}, u32[]{:S(2)}) collective-permute-start(bf16[256,256]{1,0:T(8,128)(2,1)S(1)} %get-tuple-element.35), channel_id=1, source_target_pairs={{0,224},{4,36},{8,232},{12,44},{16,240},{20,52},{24,248},{28,60},{... | collective-permute-start | bytes 393224 | tf_op jit(solution)/shard_map/ppermute | solution.py:48
  81.9 11.6 %collective-permute-start.18 = (bf16[256,256]{1,0:T(8,128)(2,1)S(1)}, bf16[256,256]{1,0:T(8,128)(2,1)S(1)}, u32[]{:S(2)}, u32[]{:S(2)}) collective-permute-start(bf16[256,256]{1,0:T(8,128)(2,1)S(1)} %get-tuple-element.36), channel_id=1, source_target_pairs={{0,192},{4,68},{8,200},{12,76},{16,208},{20,84},{24,216},{28,92},{... | collective-permute-start | bytes 393224 | tf_op jit(solution)/shard_map/ppermute | solution.py:48
  84.7 9.0 %collective-permute-start.12 = (bf16[128,1024]{1,0:T(8,128)(2,1)S(1)}, bf16[128,1024]{1,0:T(8,128)(2,1)S(1)}, u32[]{:S(2)}, u32[]{:S(2)}) collective-permute-start(bf16[128,1024]{1,0:T(8,128)(2,1)S(1)} %get-tuple-element.31), channel_id=1, source_target_pairs={{0,16},{4,20},{8,24},{12,28},{16,0},{20,4},{24,8},{28,12},{32,48},... | collective-permute-start | bytes 786440 | tf_op jit(solution)/shard_map/ppermute | solution.py:48
  85.0 15.0 %collective-permute-start.14 = (bf16[128,1024]{1,0:T(8,128)(2,1)S(1)}, bf16[128,1024]{1,0:T(8,128)(2,1)S(1)}, u32[]{:S(2)}, u32[]{:S(2)}) collective-permute-start(bf16[128,1024]{1,0:T(8,128)(2,1)S(1)} %get-tuple-element.32), channel_id=1, source_target_pairs={{0,8},{4,12},{8,16},{12,20},{16,24},{20,28},{24,0},{28,4},{32,40},... | collective-permute-start | bytes 786440 | tf_op jit(solution)/shard_map/ppermute | solution.py:48
  86.8 13.3 %collective-permute-start.13 = (bf16[128,1024]{1,0:T(8,128)(2,1)S(1)}, bf16[128,1024]{1,0:T(8,128)(2,1)S(1)}, u32[]{:S(2)}, u32[]{:S(2)}) collective-permute-start(bf16[128,1024]{1,0:T(8,128)(2,1)S(1)} %get-tuple-element.33), channel_id=1, source_target_pairs={{0,24},{4,28},{8,0},{12,4},{16,8},{20,12},{24,16},{28,20},{32,56},... | collective-permute-start | bytes 786440 | tf_op jit(solution)/shard_map/ppermute | solution.py:48
  87.7 13.2 %collective-permute-start.16 = (bf16[128,256]{1,0:T(8,128)(2,1)S(1)}, bf16[128,256]{1,0:T(8,128)(2,1)S(1)}, u32[]{:S(2)}, u32[]{:S(2)}) collective-permute-start(bf16[128,256]{1,0:T(8,128)(2,1)S(1)} %slice.102), channel_id=1, source_target_pairs={{0,128},{4,132},{8,136},{12,140},{16,144},{20,148},{24,152},{28,15... | collective-permute-start | bytes 196616 | tf_op jit(solution)/shard_map/ppermute | solution.py:48
  93.5 7.4 %collective-permute-start.20 = (bf16[128,256]{1,0:T(8,128)(2,1)S(1)}, bf16[128,256]{1,0:T(8,128)(2,1)S(1)}, u32[]{:S(2)}, u32[]{:S(2)}) collective-permute-start(bf16[128,256]{1,0:T(8,128)(2,1)S(1)} %slice.123), channel_id=1, source_target_pairs={{0,4},{4,0},{8,12},{12,8},{16,20},{20,16},{24,28},{28,24},{32,36},... | collective-permute-start | bytes 196616 | tf_op jit(solution)/shard_map/ppermute | solution.py:48
where the time goes:
time: 101 us; the launch traced here: 102 us
  starting transfers between devices  45.4 us (45%)
  Pallas kernels  26.6 us (26%)
  waiting for transfers between devices  22 us (22%)
  other arithmetic  3.76 us (4%)
  local copies, waits for them, and re-layouts  3.04 us (3%)
    ppermute x21, starting transfers between devices, send(): return lax.ppermute(x, AXES, moves(fn))  45.4 us
    pallas_call x2, Pallas kernels, run(): pl.pallas_call(body, out_shape=outs, in_specs=[smem] + [vmem] * len(args)...  26.6 us
    ppermute x21, waiting for transfers between devices, send(): return lax.ppermute(x, AXES, moves(fn))  22 us
  transfers between devices with their start and end apart: 21, of which 10 were waited for; matrix products, arithmetic and copies ran while one was open for 2% of the time, Pallas kernels for 0%

commit v1 on v0

--- a/solution.py
+++ b/solution.py
@@ -119,6 +119,16 @@
     lax.fori_loop(0, fulls, lambda j, _: step(whole * PER, CH, True), 0)
 
 
+def walk_wide(meta, qb, step):
+    whole = meta[2 * KB + qb]
+    halves = meta[2 * KB + QB + qb]
+    fulls = meta[2 * KB + 2 * QB + qb]
+    lax.fori_loop(0, whole // 2, lambda j, _: step(j * 2 * PER, 2 * CH, False), 0)
+    lax.fori_loop(0, whole % 2, lambda j, _: step((whole - 1) * PER, CH, False), 0)
+    lax.fori_loop(0, halves, lambda j, _: step(whole * PER, CH // 2, True), 0)
+    lax.fori_loop(0, fulls, lambda j, _: step(whole * PER, CH, True), 0)
+
+
 def query_rows(qb):
     return pl.ds(pl.multiple_of(qb * ROWS, ROWS), ROWS)
 
@@ -238,7 +248,7 @@
             qacc[qb] += dot_nn(kt[:, at], ds)
             return 0
 
-        walk(meta, qb, step)
+        walk_wide(meta, qb, step)
         return 0
 
     lax.fori_loop(0, QB, block, 0)
@@ -331,18 +341,18 @@
 
 
 def on_device(query_states, key_states, value_states, output_grad, positions):
-    own_ids = (positions[::SPAN] // SPAN).astype(BF16)
+    ids = (positions // SPAN).astype(BF16)
     kv = jnp.concatenate(
         [
             jnp.concatenate([key_states, value_states], axis=1),
-            jnp.broadcast_to(jnp.repeat(own_ids, HD)[None, :], (16, 2 * HD)),
+            jnp.broadcast_to(jnp.tile(ids, 2)[None, :], (16, 2 * HD)),
         ],
         axis=0,
     )
     qg = jnp.concatenate(
         [
             query_states,
-            jnp.broadcast_to(jnp.repeat(own_ids, 4 * HD)[None, :], (16, HQ * HD)),
+            jnp.broadcast_to(jnp.tile(ids, HQ)[None, :], (16, HQ * HD)),
             output_grad,
         ],
         axis=0,
@@ -363,12 +373,10 @@
     xb = send(kb, to_core)
 
     def ids_of(x):
-        return x.reshape(-1, SHARD, 2 * HD)[:, TOK, ::HD].reshape(-1)
+        return x.reshape(-1, SHARD, 2 * HD)[:, TOK, 0:HD:SPAN].reshape(-1)
 
     kid = jnp.concatenate([ids_of(x) for x in (pair, ka, kb, xa, xb)]).astype(jnp.int32)
-    qid = jnp.concatenate(
-        [own_ids] + [x[TOK, :: 4 * HD] for x in (qa, qb, qc)]
-    ).astype(jnp.int32)
+    qid = jnp.concatenate([ids[::SPAN]] + [x[TOK, 0:HD:SPAN] for x in (qa, qb, qc)]).astype(jnp.int32)
     rank = jnp.sum((kid[None, :] < kid[:, None]).astype(jnp.int32), axis=1)
     slots = jnp.arange(KB, dtype=jnp.int32)
     in_order = jnp.sum(jnp.where(rank[None, :] == slots[:, None], kid[None, :], 0), axis=1)

time: 101 us -> 100 us (0.990); the launches traced: 102 us -> 102 us
  Pallas kernels: 26.6 us -> 21.1 us
  starting transfers between devices: 45.4 us -> 48.7 us
  waiting for transfers between devices: 22 us -> 24.5 us
    pallas_call x2, Pallas kernels: 26.6 us -> 21.1 us  [run(): pl.pallas_call(body, out_shape=outs, in_specs=[smem] + [vmem] * len(args)...]
    ppermute x21, starting transfers between devices: 45.4 us -> 48.7 us  [send(): return lax.ppermute(x, AXES, moves(fn))]
    ppermute x21, waiting for transfers between devices: 22 us -> 24.5 us  [send(): return lax.ppermute(x, AXES, moves(fn))]
  transfers between devices with their start and end apart: 21 -> 21, of which waited for: 10 -> 11; matrix products, arithmetic and copies ran while one was open for 2% -> 2% of each run, Pallas kernels for 0% -> 0%
where the time goes in v1:
time: 100 us; the launch traced here: 102 us
  starting transfers between devices  48.7 us (49%)
  waiting for transfers between devices  24.5 us (24%)
  Pallas kernels  21.1 us (21%)
  other arithmetic  4.42 us (4%)
  local copies, waits for them, and re-layouts  2.23 us (2%)
    ppermute x21, starting transfers between devices, send(): return lax.ppermute(x, AXES, moves(fn))  48.7 us
    ppermute x21, waiting for transfers between devices, send(): return lax.ppermute(x, AXES, moves(fn))  24.5 us
    pallas_call x2, Pallas kernels, run(): pl.pallas_call(body, out_shape=outs, in_specs=[smem] + [vmem] * len(args)...  21.1 us
  transfers between devices with their start and end apart: 21, of which 11 were waited for; matrix products, arithmetic and copies ran while one was open for 2% of the time, Pallas kernels for 0%

profile of v1, /device:TPU:1, one launch (start us, length us, event | category | flops | bytes accessed | tf_op | source)
XLA Modules:
  0.0 101.7 jit_solution(5634653005413611408)
XLA Ops:
  0.6 0.7 fusion.5
  1.3 0.8 pad_maximum_fusion.2
  2.1 1.1 %pad_maximum_fusion = bf16[272,1024]{1,0:T(8,128)(2,1)S(1)} fusion(bf16[128,1024]{1,0:T(8,128)(2,1)} %g0.3, bf16[16,1024]{1,0:T(8,128)(2,1)S(1)} %broadcast_in_dim.19, bf16[128,1024]{1,0:T(8,128)(2,1)} %q0.3), kind=kLoop, calls=%fused_computation.1 | loop fusion | flops 1671168 | bytes 1114112 | tf_op jit(solution)/shard_map/concatenate | solution.py:352
  3.2 3.6 %collective-permute-start.2 = (bf16[272,1024]{1,0:T(8,128)(2,1)S(1)}, bf16[272,1024]{1,0:T(8,128)(2,1)S(1)}, u32[]{:S(2)}, u32[]{:S(2)}) collective-permute-start(bf16[272,1024]{1,0:T(8,128)(2,1)S(1)} %pad_maximum_fusion), channel_id=1, source_target_pairs={{0,24},{4,28},{8,0},{12,4},{16,8},{20,12},{24,16},{28,20},{32,56},... | collective-permute-start | bytes 1671176 | tf_op jit(solution)/shard_map/ppermute | solution.py:48
  6.8 0.0 collective-permute-start.1
  6.8 1.7 %collective-permute-start = (bf16[144,256]{1,0:T(8,128)(2,1)S(1)}, bf16[144,256]{1,0:T(8,128)(2,1)S(1)}, u32[]{:S(2)}, u32[]{:S(2)}) collective-permute-start(bf16[144,256]{1,0:T(8,128)(2,1)S(1)} %pad_maximum_fusion.2), channel_id=1, source_target_pairs={{0,4},{4,0},{8,12},{12,8},{16,20},{20,16},{24,28},{28,24},{32,36},... | collective-permute-start | bytes 221192 | tf_op jit(solution)/shard_map/ppermute | solution.py:48
  8.5 0.9 collective-permute-done
  9.5 5.7 %collective-permute-start.4 = (bf16[288,256]{1,0:T(8,128)(2,1)S(1)}, bf16[288,256]{1,0:T(8,128)(2,1)S(1)}, u32[]{:S(2)}, u32[]{:S(2)}) collective-permute-start(bf16[288,256]{1,0:T(8,128)(2,1)S(1)} %constant_dynamic-update-slice_fusion.own), channel_id=1, source_target_pairs={{0,96},{4,164},{8,104},{12,172},{16,112},{20,180},{24,120},{28,188... | collective-permute-start | bytes 442376 | tf_op jit(solution)/shard_map/ppermute | solution.py:48
  15.2 0.7 collective-permute-start.3
  15.9 4.5 %collective-permute-done.4 = bf16[288,256]{1,0:T(8,128)(2,1)S(1)} collective-permute-done((bf16[288,256]{1,0:T(8,128)(2,1)S(1)}, bf16[288,256]{1,0:T(8,128)(2,1)S(1)}, u32[]{:S(2)}, u32[]{:S(2)}) %collective-permute-start.4) | collective-permute-done | bytes 147488 | tf_op jit(solution)/shard_map/ppermute | solution.py:48
  20.4 1.6 %collective-permute-done.3 = bf16[288,256]{1,0:T(8,128)(2,1)S(1)} collective-permute-done((bf16[288,256]{1,0:T(8,128)(2,1)S(1)}, bf16[288,256]{1,0:T(8,128)(2,1)S(1)}, u32[]{:S(2)}, u32[]{:S(2)}) %collective-permute-start.3) | collective-permute-done | bytes 147488 | tf_op jit(solution)/shard_map/ppermute | solution.py:48
  22.0 0.1 broadcast_select_fusion
  22.1 0.0 copy-start
  22.1 0.0 copy-start.1
  22.1 3.0 %collective-permute-start.6 = (bf16[272,1024]{1,0:T(8,128)(2,1)S(1)}, bf16[272,1024]{1,0:T(8,128)(2,1)S(1)}, u32[]{:S(2)}, u32[]{:S(2)}) collective-permute-start(bf16[272,1024]{1,0:T(8,128)(2,1)S(1)} %broadcast_select_fusion), channel_id=1, source_target_pairs={{0,8},{4,28},{8,16},{12,4},{16,24},{20,12},{24,0},{28,20},{32,40},... | collective-permute-start | bytes 1671176 | tf_op jit(solution)/shard_map/ppermute | solution.py:48
  25.2 3.4 %collective-permute-start.5 = (bf16[432,256]{1,0:T(8,128)(2,1)S(1)}, bf16[432,256]{1,0:T(8,128)(2,1)S(1)}, u32[]{:S(2)}, u32[]{:S(2)}) collective-permute-start(bf16[432,256]{1,0:T(8,128)(2,1)S(1)} %pad_maximum_fusion.1), channel_id=1, source_target_pairs={{0,32},{4,228},{8,40},{12,236},{16,48},{20,244},{24,56},{28,252},{... | collective-permute-start | bytes 663560 | tf_op jit(solution)/shard_map/ppermute | solution.py:48
  28.6 0.1 collective-permute-start.7
  28.7 2.7 %collective-permute-done.5.kb = bf16[432,256]{1,0:T(8,128)(2,1)S(1)} collective-permute-done((bf16[432,256]{1,0:T(8,128)(2,1)S(1)}, bf16[432,256]{1,0:T(8,128)(2,1)S(1)}, u32[]{:S(2)}, u32[]{:S(2)}) %collective-permute-start.5) | collective-permute-done | bytes 221216 | tf_op jit(solution)/shard_map/ppermute | solution.py:48
  31.4 0.2 collective-permute-done.6.qc
  31.6 2.4 %collective-permute-start.8 = (bf16[432,256]{1,0:T(8,128)(2,1)S(1)}, bf16[432,256]{1,0:T(8,128)(2,1)S(1)}, u32[]{:S(2)}, u32[]{:S(2)}) collective-permute-start(bf16[432,256]{1,0:T(8,128)(2,1)S(1)} %collective-permute-done.5.kb), channel_id=1, source_target_pairs={{0,4},{4,0},{8,12},{12,8},{16,20},{20,16},{24,28},{28,24},{32,36},... | collective-permute-start | bytes 663560 | tf_op jit(solution)/shard_map/ppermute | solution.py:48
  34.0 0.1 slice.84
  34.1 0.1 slice.78
  34.2 0.1 concatenate.59
  34.3 0.1 slice.85
  34.4 0.1 slice.86
  34.5 0.1 slice.79
  34.6 0.1 concatenate.61
  34.7 0.1 slice.82
  34.8 0.1 concatenate.64
  34.9 0.1 slice.87
  35.0 0.1 slice.81
  35.1 0.1 concatenate.63
  35.2 0.1 maximum_convert_fusion
  35.3 0.1 slice.83
  35.4 0.1 concatenate.65
  35.5 0.1 concatenate.66
  35.6 0.2 convert_reduce_fusion
  35.8 0.1 select_reduce_fusion
  35.9 0.2 convert_reduce_fusion.1
  36.1 0.1 concatenate.71.meta
  36.2 8.0 %shard_map.76.st0 = f32[3,8,512]{2,1,0:T(8,128)S(1)} custom-call(s32[96]{0:T(128)S(1)} %concatenate.71.meta, bf16[288,256]{1,0:T(8,128)(2,1)S(1)} %constant_dynamic-update-slice_fusion.own, bf16[576,256]{1,0:T(8,128)(2,1)S(1)} %constant_dynamic-update-slice_fusion.2.ka, bf16[432,256]{1,0:T(8,128)(2,1)S(1)} %collective-permute-done.5.kb, ...), custom_call_target="tpu_custom_call" | custom-call | flops 2147483648 | bytes 6291456 | tf_op jit(solution)/shard_map/pallas_call | solution.py:281
  44.2 0.5 collective-permute-start.11
  44.8 2.2 %collective-permute-start.10 = (f32[3,8,512]{2,1,0:T(8,128)S(1)}, f32[3,8,512]{2,1,0:T(8,128)S(1)}, u32[]{:S(2)}, u32[]{:S(2)}) collective-permute-start(f32[3,8,512]{2,1,0:T(8,128)S(1)} %shard_map.76.st0), channel_id=1, source_target_pairs={{0,24},{4,28},{8,0},{12,4},{16,8},{20,12},{24,16},{28,20},{32,56},... | collective-permute-start | bytes 147464 | tf_op jit(solution)/shard_map/ppermute | solution.py:48
  47.0 0.5 collective-permute-start.9
  47.5 1.3 %collective-permute-done.11.stc = f32[3,8,512]{2,1,0:T(8,128)S(1)} collective-permute-done((f32[3,8,512]{2,1,0:T(8,128)S(1)}, f32[3,8,512]{2,1,0:T(8,128)S(1)}, u32[]{:S(2)}, u32[]{:S(2)}) %collective-permute-start.11) | collective-permute-done | bytes 49184 | tf_op jit(solution)/shard_map/ppermute | solution.py:48
  48.8 0.7 collective-permute-done.10.stb
  49.5 1.7 %collective-permute-done.9.sta = f32[3,8,512]{2,1,0:T(8,128)S(1)} collective-permute-done((f32[3,8,512]{2,1,0:T(8,128)S(1)}, f32[3,8,512]{2,1,0:T(8,128)S(1)}, u32[]{:S(2)}, u32[]{:S(2)}) %collective-permute-start.9) | collective-permute-done | bytes 49184 | tf_op jit(solution)/shard_map/ppermute | solution.py:48
  51.1 13.1 %shard_map.77 = (bf16[4,128,1024]{2,1,0:T(8,128)(2,1)S(1)}, bf16[1024,256]{1,0:T(8,128)(2,1)S(1)}, bf16[1024,256]{1,0:T(8,128)(2,1)S(1)}) custom-call(s32[96]{0:T(128)S(1)} %concatenate.71.meta, bf16[288,256]{1,0:T(8,128)(2,1)S(1)} %constant_dynamic-update-slice_fusion.own, bf16[576,256]{1,0:T(8,128)(2,1)S(1)} %constant_dynamic-update-slice_fusion.2.ka, ...), custom_call_target="tpu_custom_call" | custom-call | flops 5368709120 | bytes 6291456 | tf_op jit(solution)/shard_map/pallas_call | solution.py:281
  64.2 12.0 %collective-permute-start.15 = (bf16[1024,256]{1,0:T(8,128)(2,1)S(1)}, bf16[1024,256]{1,0:T(8,128)(2,1)S(1)}, u32[]{:S(2)}, u32[]{:S(2)}) collective-permute-start(bf16[1024,256]{1,0:T(8,128)(2,1)S(1)} %get-tuple-element.24), channel_id=1, source_target_pairs={{0,4},{4,0},{8,12},{12,8},{16,20},{20,16},{24,28},{28,24},{32,36},... | collective-permute-start | bytes 1572872 | tf_op jit(solution)/shard_map/ppermute | solution.py:48
  76.2 1.5 %collective-permute-done.15 = bf16[1024,256]{1,0:T(8,128)(2,1)S(1)} collective-permute-done((bf16[1024,256]{1,0:T(8,128)(2,1)S(1)}, bf16[1024,256]{1,0:T(8,128)(2,1)S(1)}, u32[]{:S(2)}, u32[]{:S(2)}) %collective-permute-start.15) | collective-permute-done | bytes 524320 | tf_op jit(solution)/shard_map/ppermute | solution.py:48
  77.8 0.2 convert_add_fusion
  78.0 0.1 collective-permute-start.17
  78.1 0.1 collective-permute-start.19
  78.1 7.0 %collective-permute-start.18 = (bf16[256,256]{1,0:T(8,128)(2,1)S(1)}, bf16[256,256]{1,0:T(8,128)(2,1)S(1)}, u32[]{:S(2)}, u32[]{:S(2)}) collective-permute-start(bf16[256,256]{1,0:T(8,128)(2,1)S(1)} %get-tuple-element.36), channel_id=1, source_target_pairs={{0,192},{4,68},{8,200},{12,76},{16,208},{20,84},{24,216},{28,92},{... | collective-permute-start | bytes 393224 | tf_op jit(solution)/shard_map/ppermute | solution.py:48
  85.1 0.1 slice_bitcast_fusion.2
  85.2 0.1 collective-permute-start.12
  85.3 1.3 %collective-permute-start.14 = (bf16[128,1024]{1,0:T(8,128)(2,1)S(1)}, bf16[128,1024]{1,0:T(8,128)(2,1)S(1)}, u32[]{:S(2)}, u32[]{:S(2)}) collective-permute-start(bf16[128,1024]{1,0:T(8,128)(2,1)S(1)} %get-tuple-element.32), channel_id=1, source_target_pairs={{0,8},{4,12},{8,16},{12,20},{16,24},{20,28},{24,0},{28,4},{32,40},... | collective-permute-start | bytes 786440 | tf_op jit(solution)/shard_map/ppermute | solution.py:48
  86.6 1.5 %collective-permute-start.13 = (bf16[128,1024]{1,0:T(8,128)(2,1)S(1)}, bf16[128,1024]{1,0:T(8,128)(2,1)S(1)}, u32[]{:S(2)}, u32[]{:S(2)}) collective-permute-start(bf16[128,1024]{1,0:T(8,128)(2,1)S(1)} %get-tuple-element.33), channel_id=1, source_target_pairs={{0,24},{4,28},{8,0},{12,4},{16,8},{20,12},{24,16},{28,20},{32,56},... | collective-permute-start | bytes 786440 | tf_op jit(solution)/shard_map/ppermute | solution.py:48
  88.0 0.6 collective-permute-start.16
  88.7 2.2 %collective-permute-start.20 = (bf16[128,256]{1,0:T(8,128)(2,1)S(1)}, bf16[128,256]{1,0:T(8,128)(2,1)S(1)}, u32[]{:S(2)}, u32[]{:S(2)}) collective-permute-start(bf16[128,256]{1,0:T(8,128)(2,1)S(1)} %slice.123), channel_id=1, source_target_pairs={{0,4},{4,0},{8,12},{12,8},{16,20},{20,16},{24,28},{28,24},{32,36},... | collective-permute-start | bytes 196616 | tf_op jit(solution)/shard_map/ppermute | solution.py:48
  90.9 3.9 %collective-permute-done.12 = bf16[128,1024]{1,0:T(8,128)(2,1)S(1)} collective-permute-done((bf16[128,1024]{1,0:T(8,128)(2,1)S(1)}, bf16[128,1024]{1,0:T(8,128)(2,1)S(1)}, u32[]{:S(2)}, u32[]{:S(2)}) %collective-permute-start.12) | collective-permute-done | bytes 262176 | tf_op jit(solution)/shard_map/ppermute | solution.py:48
  94.8 5.4 %collective-permute-done.14 = bf16[128,1024]{1,0:T(8,128)(2,1)S(1)} collective-permute-done((bf16[128,1024]{1,0:T(8,128)(2,1)S(1)}, bf16[128,1024]{1,0:T(8,128)(2,1)S(1)}, u32[]{:S(2)}, u32[]{:S(2)}) %collective-permute-start.14) | collective-permute-done | bytes 262176 | tf_op jit(solution)/shard_map/ppermute | solution.py:48
  100.2 0.9 fusion.2
  101.1 0.6 fusion.8
  (35 shorter events, 0.4 us)
Async XLA Ops:
  3.2 18.8 %collective-permute-start.2 = (bf16[272,1024]{1,0:T(8,128)(2,1)S(1)}, bf16[272,1024]{1,0:T(8,128)(2,1)S(1)}, u32[]{:S(2)}, u32[]{:S(2)}) collective-permute-start(bf16[272,1024]{1,0:T(8,128)(2,1)S(1)} %pad_maximum_fusion), channel_id=1, source_target_pairs={{0,24},{4,28},{8,0},{12,4},{16,8},{20,12},{24,16},{28,20},{32,56},... | collective-permute-start | bytes 1671176 | tf_op jit(solution)/shard_map/ppermute | solution.py:48
  6.8 15.2 %collective-permute-start.1 = (bf16[272,1024]{1,0:T(8,128)(2,1)S(1)}, bf16[272,1024]{1,0:T(8,128)(2,1)S(1)}, u32[]{:S(2)}, u32[]{:S(2)}) collective-permute-start(bf16[272,1024]{1,0:T(8,128)(2,1)S(1)} %pad_maximum_fusion), channel_id=1, source_target_pairs={{0,8},{4,12},{8,16},{12,20},{16,24},{20,28},{24,0},{28,4},{32,40},... | collective-permute-start | bytes 1671176 | tf_op jit(solution)/shard_map/ppermute | solution.py:48
  6.8 2.6 %collective-permute-start = (bf16[144,256]{1,0:T(8,128)(2,1)S(1)}, bf16[144,256]{1,0:T(8,128)(2,1)S(1)}, u32[]{:S(2)}, u32[]{:S(2)}) collective-permute-start(bf16[144,256]{1,0:T(8,128)(2,1)S(1)} %pad_maximum_fusion.2), channel_id=1, source_target_pairs={{0,4},{4,0},{8,12},{12,8},{16,20},{20,16},{24,28},{28,24},{32,36},... | collective-permute-start | bytes 221192 | tf_op jit(solution)/shard_map/ppermute | solution.py:48
  9.5 11.0 %collective-permute-start.4 = (bf16[288,256]{1,0:T(8,128)(2,1)S(1)}, bf16[288,256]{1,0:T(8,128)(2,1)S(1)}, u32[]{:S(2)}, u32[]{:S(2)}) collective-permute-start(bf16[288,256]{1,0:T(8,128)(2,1)S(1)} %constant_dynamic-update-slice_fusion.own), channel_id=1, source_target_pairs={{0,96},{4,164},{8,104},{12,172},{16,112},{20,180},{24,120},{28,188... | collective-permute-start | bytes 442376 | tf_op jit(solution)/shard_map/ppermute | solution.py:48
  15.2 6.8 %collective-permute-start.3 = (bf16[288,256]{1,0:T(8,128)(2,1)S(1)}, bf16[288,256]{1,0:T(8,128)(2,1)S(1)}, u32[]{:S(2)}, u32[]{:S(2)}) collective-permute-start(bf16[288,256]{1,0:T(8,128)(2,1)S(1)} %constant_dynamic-update-slice_fusion.own), channel_id=1, source_target_pairs={{0,32},{4,228},{8,40},{12,236},{16,48},{20,244},{24,56},{28,252},{... | collective-permute-start | bytes 442376 | tf_op jit(solution)/shard_map/ppermute | solution.py:48
  22.1 14.1 %copy-start = (bf16[128,1024]{1,0:T(8,128)(2,1)S(1)}, bf16[128,1024]{1,0:T(8,128)(2,1)}, u32[]{:S(2)}) copy-start(bf16[128,1024]{1,0:T(8,128)(2,1)} %g0.3) | copy-start | bytes 786436
  22.1 14.1 %copy-start.1 = (bf16[128,1024]{1,0:T(8,128)(2,1)S(1)}, bf16[128,1024]{1,0:T(8,128)(2,1)}, u32[]{:S(2)}) copy-start(bf16[128,1024]{1,0:T(8,128)(2,1)} %q0.3) | copy-start | bytes 786436
  22.1 9.5 %collective-permute-start.6 = (bf16[272,1024]{1,0:T(8,128)(2,1)S(1)}, bf16[272,1024]{1,0:T(8,128)(2,1)S(1)}, u32[]{:S(2)}, u32[]{:S(2)}) collective-permute-start(bf16[272,1024]{1,0:T(8,128)(2,1)S(1)} %broadcast_select_fusion), channel_id=1, source_target_pairs={{0,8},{4,28},{8,16},{12,4},{16,24},{20,12},{24,0},{28,20},{32,40},... | collective-permute-start | bytes 1671176 | tf_op jit(solution)/shard_map/ppermute | solution.py:48
  25.2 6.3 %collective-permute-start.5 = (bf16[432,256]{1,0:T(8,128)(2,1)S(1)}, bf16[432,256]{1,0:T(8,128)(2,1)S(1)}, u32[]{:S(2)}, u32[]{:S(2)}) collective-permute-start(bf16[432,256]{1,0:T(8,128)(2,1)S(1)} %pad_maximum_fusion.1), channel_id=1, source_target_pairs={{0,32},{4,228},{8,40},{12,236},{16,48},{20,244},{24,56},{28,252},{... | collective-permute-start | bytes 663560 | tf_op jit(solution)/shard_map/ppermute | solution.py:48
  28.6 6.1 %collective-permute-start.7 = (bf16[576,256]{1,0:T(8,128)(2,1)S(1)}, bf16[576,256]{1,0:T(8,128)(2,1)S(1)}, u32[]{:S(2)}, u32[]{:S(2)}) collective-permute-start(bf16[576,256]{1,0:T(8,128)(2,1)S(1)} %constant_dynamic-update-slice_fusion.2.ka), channel_id=1, source_target_pairs={{0,4},{4,0},{8,12},{12,8},{16,20},{20,16},{24,28},{28,24},{32,36},... | collective-permute-start | bytes 884744 | tf_op jit(solution)/shard_map/ppermute | solution.py:48
  31.6 3.6 %collective-permute-start.8 = (bf16[432,256]{1,0:T(8,128)(2,1)S(1)}, bf16[432,256]{1,0:T(8,128)(2,1)S(1)}, u32[]{:S(2)}, u32[]{:S(2)}) collective-permute-start(bf16[432,256]{1,0:T(8,128)(2,1)S(1)} %collective-permute-done.5.kb), channel_id=1, source_target_pairs={{0,4},{4,0},{8,12},{12,8},{16,20},{20,16},{24,28},{28,24},{32,36},... | collective-permute-start | bytes 663560 | tf_op jit(solution)/shard_map/ppermute | solution.py:48
  44.2 4.5 %collective-permute-start.11 = (f32[3,8,512]{2,1,0:T(8,128)S(1)}, f32[3,8,512]{2,1,0:T(8,128)S(1)}, u32[]{:S(2)}, u32[]{:S(2)}) collective-permute-start(f32[3,8,512]{2,1,0:T(8,128)S(1)} %shard_map.76.st0), channel_id=1, source_target_pairs={{0,16},{4,20},{8,24},{12,28},{16,0},{20,4},{24,8},{28,12},{32,48},... | collective-permute-start | bytes 147464 | tf_op jit(solution)/shard_map/ppermute | solution.py:48
  44.8 4.7 %collective-permute-start.10 = (f32[3,8,512]{2,1,0:T(8,128)S(1)}, f32[3,8,512]{2,1,0:T(8,128)S(1)}, u32[]{:S(2)}, u32[]{:S(2)}) collective-permute-start(f32[3,8,512]{2,1,0:T(8,128)S(1)} %shard_map.76.st0), channel_id=1, source_target_pairs={{0,24},{4,28},{8,0},{12,4},{16,8},{20,12},{24,16},{28,20},{32,56},... | collective-permute-start | bytes 147464 | tf_op jit(solution)/shard_map/ppermute | solution.py:48
  47.0 4.2 %collective-permute-start.9 = (f32[3,8,512]{2,1,0:T(8,128)S(1)}, f32[3,8,512]{2,1,0:T(8,128)S(1)}, u32[]{:S(2)}, u32[]{:S(2)}) collective-permute-start(f32[3,8,512]{2,1,0:T(8,128)S(1)} %shard_map.76.st0), channel_id=1, source_target_pairs={{0,8},{4,12},{8,16},{12,20},{16,24},{20,28},{24,0},{28,4},{32,40},... | collective-permute-start | bytes 147464 | tf_op jit(solution)/shard_map/ppermute | solution.py:48
  64.2 13.5 %collective-permute-start.15 = (bf16[1024,256]{1,0:T(8,128)(2,1)S(1)}, bf16[1024,256]{1,0:T(8,128)(2,1)S(1)}, u32[]{:S(2)}, u32[]{:S(2)}) collective-permute-start(bf16[1024,256]{1,0:T(8,128)(2,1)S(1)} %get-tuple-element.24), channel_id=1, source_target_pairs={{0,4},{4,0},{8,12},{12,8},{16,20},{20,16},{24,28},{28,24},{32,36},... | collective-permute-start | bytes 1572872 | tf_op jit(solution)/shard_map/ppermute | solution.py:48
  78.0 8.6 %collective-permute-start.17 = (bf16[256,256]{1,0:T(8,128)(2,1)S(1)}, bf16[256,256]{1,0:T(8,128)(2,1)S(1)}, u32[]{:S(2)}, u32[]{:S(2)}) collective-permute-start(bf16[256,256]{1,0:T(8,128)(2,1)S(1)} %get-tuple-element.34), channel_id=1, source_target_pairs={{0,160},{4,100},{8,168},{12,108},{16,176},{20,116},{24,184},{28,12... | collective-permute-start | bytes 393224 | tf_op jit(solution)/shard_map/ppermute | solution.py:48
  78.1 10.0 %collective-permute-start.19 = (bf16[256,256]{1,0:T(8,128)(2,1)S(1)}, bf16[256,256]{1,0:T(8,128)(2,1)S(1)}, u32[]{:S(2)}, u32[]{:S(2)}) collective-permute-start(bf16[256,256]{1,0:T(8,128)(2,1)S(1)} %get-tuple-element.35), channel_id=1, source_target_pairs={{0,224},{4,36},{8,232},{12,44},{16,240},{20,52},{24,248},{28,60},{... | collective-permute-start | bytes 393224 | tf_op jit(solution)/shard_map/ppermute | solution.py:48
  78.1 10.4 %collective-permute-start.18 = (bf16[256,256]{1,0:T(8,128)(2,1)S(1)}, bf16[256,256]{1,0:T(8,128)(2,1)S(1)}, u32[]{:S(2)}, u32[]{:S(2)}) collective-permute-start(bf16[256,256]{1,0:T(8,128)(2,1)S(1)} %get-tuple-element.36), channel_id=1, source_target_pairs={{0,192},{4,68},{8,200},{12,76},{16,208},{20,84},{24,216},{28,92},{... | collective-permute-start | bytes 393224 | tf_op jit(solution)/shard_map/ppermute | solution.py:48
  85.2 9.6 %collective-permute-start.12 = (bf16[128,1024]{1,0:T(8,128)(2,1)S(1)}, bf16[128,1024]{1,0:T(8,128)(2,1)S(1)}, u32[]{:S(2)}, u32[]{:S(2)}) collective-permute-start(bf16[128,1024]{1,0:T(8,128)(2,1)S(1)} %get-tuple-element.31), channel_id=1, source_target_pairs={{0,16},{4,20},{8,24},{12,28},{16,0},{20,4},{24,8},{28,12},{32,48},... | collective-permute-start | bytes 786440 | tf_op jit(solution)/shard_map/ppermute | solution.py:48
  85.3 14.9 %collective-permute-start.14 = (bf16[128,1024]{1,0:T(8,128)(2,1)S(1)}, bf16[128,1024]{1,0:T(8,128)(2,1)S(1)}, u32[]{:S(2)}, u32[]{:S(2)}) collective-permute-start(bf16[128,1024]{1,0:T(8,128)(2,1)S(1)} %get-tuple-element.32), channel_id=1, source_target_pairs={{0,8},{4,12},{8,16},{12,20},{16,24},{20,28},{24,0},{28,4},{32,40},... | collective-permute-start | bytes 786440 | tf_op jit(solution)/shard_map/ppermute | solution.py:48
  86.6 13.6 %collective-permute-start.13 = (bf16[128,1024]{1,0:T(8,128)(2,1)S(1)}, bf16[128,1024]{1,0:T(8,128)(2,1)S(1)}, u32[]{:S(2)}, u32[]{:S(2)}) collective-permute-start(bf16[128,1024]{1,0:T(8,128)(2,1)S(1)} %get-tuple-element.33), channel_id=1, source_target_pairs={{0,24},{4,28},{8,0},{12,4},{16,8},{20,12},{24,16},{28,20},{32,56},... | collective-permute-start | bytes 786440 | tf_op jit(solution)/shard_map/ppermute | solution.py:48
  88.0 13.0 %collective-permute-start.16 = (bf16[128,256]{1,0:T(8,128)(2,1)S(1)}, bf16[128,256]{1,0:T(8,128)(2,1)S(1)}, u32[]{:S(2)}, u32[]{:S(2)}) collective-permute-start(bf16[128,256]{1,0:T(8,128)(2,1)S(1)} %slice.102), channel_id=1, source_target_pairs={{0,128},{4,132},{8,136},{12,140},{16,144},{20,148},{24,152},{28,15... | collective-permute-start | bytes 196616 | tf_op jit(solution)/shard_map/ppermute | solution.py:48
  88.7 12.4 %collective-permute-start.20 = (bf16[128,256]{1,0:T(8,128)(2,1)S(1)}, bf16[128,256]{1,0:T(8,128)(2,1)S(1)}, u32[]{:S(2)}, u32[]{:S(2)}) collective-permute-start(bf16[128,256]{1,0:T(8,128)(2,1)S(1)} %slice.123), channel_id=1, source_target_pairs={{0,4},{4,0},{8,12},{12,8},{16,20},{20,16},{24,28},{28,24},{32,36},... | collective-permute-start | bytes 196616 | tf_op jit(solution)/shard_map/ppermute | solution.py:48

commit v2 on v1

--- a/solution.py
+++ b/solution.py
@@ -26,6 +26,7 @@
 SCALE2 = SCALE * 1.4426950408889634
 NEG = -1e30
 VMEM_LIMIT = 48 * 1024 * 1024
+PACK_LIMIT = 60 * 1024 * 1024
 FROM_BELOW = (2, 0, 3, 1)
 FROM_ABOVE = (1, 3, 0, 2)
 FROM_FAR = (3, 2, 1, 0)
@@ -273,7 +274,7 @@
             ref[row:row + SPAN, HD:2 * HD] = dv[src, :].astype(BF16)
 
 
-def call(body, outs, scratch, flops):
+def call(body, outs, scratch, flops, limit=VMEM_LIMIT):
     vmem = pl.BlockSpec(memory_space=pltpu.VMEM)
     smem = pl.BlockSpec(memory_space=pltpu.SMEM)
 
@@ -284,7 +285,7 @@
             in_specs=[smem] + [vmem] * len(args),
             out_specs=jax.tree.map(lambda _: vmem, outs),
             scratch_shapes=scratch,
-            compiler_params=pltpu.CompilerParams(vmem_limit_bytes=VMEM_LIMIT),
+            compiler_params=pltpu.CompilerParams(vmem_limit_bytes=limit),
             cost_estimate=pl.CostEstimate(
                 flops=flops, bytes_accessed=6 * 1024 * 1024, transcendentals=QB * ROWS * KEYS // 2
             ),
@@ -295,6 +296,25 @@
 
 def shape(*dims, dtype=BF16):
     return jax.ShapeDtypeStruct(dims, dtype)
+
+
+def pack_kernel(positions, q, k, v, g, kv, qg):
+    def numbers(width):
+        lane = lax.broadcasted_iota(jnp.int32, (16, width), 1) % TOK
+        first, second = (lax.div(positions[b * SPAN], SPAN) for b in range(2))
+        return jnp.where(lane < SPAN, first, second).astype(F32).astype(BF16)
+
+    kv[0:TOK, 0:HD] = k[...]
+    kv[0:TOK, HD:2 * HD] = v[...]
+    kv[TOK:SHARD, :] = numbers(2 * HD)
+    qg[0:TOK, :] = q[...]
+    qg[TOK:SHARD, :] = numbers(HQ * HD)
+    qg[SHARD:SHARD + TOK, :] = g[...]
+
+
+def pack_call(*args):
+    outs = (shape(SHARD, 2 * HD), shape(SHARD + TOK, HQ * HD))
+    return call(pack_kernel, outs, [], 0, PACK_LIMIT)(*args)
 
 
 def fwd_call(meta, *args):
@@ -342,22 +362,7 @@
 
 def on_device(query_states, key_states, value_states, output_grad, positions):
     ids = (positions // SPAN).astype(BF16)
-    kv = jnp.concatenate(
-        [
-            jnp.concatenate([key_states, value_states], axis=1),
-            jnp.broadcast_to(jnp.tile(ids, 2)[None, :], (16, 2 * HD)),
-        ],
-        axis=0,
-    )
-    qg = jnp.concatenate(
-        [
-            query_states,
-            jnp.broadcast_to(jnp.tile(ids, HQ)[None, :], (16, HQ * HD)),
-            output_grad,
-        ],
-        axis=0,
-    )
-    qg, kv = lax.optimization_barrier((qg, kv))
+    kv, qg = pack_call(positions, query_states, key_states, value_states, output_grad)
     qa = send(qg, along_y(1))
     qb = send(qg, along_y(-1))
     pair = jnp.concatenate([kv, send(kv, to_core)], axis=0)

time: 100 us -> 101 us (1.010)
  Pallas kernels: 21.1 us -> 29.4 us
  starting transfers between devices: 48.7 us -> 40.9 us
  other arithmetic: 4.42 us -> 1.91 us
  waiting for transfers between devices: 24.5 us -> 25.8 us
    pallas_call x2 -> x3, Pallas kernels: 21.1 us -> 29.4 us  [run(): pl.pallas_call(body, out_shape=outs, in_specs=[smem] + [vmem] * len(args)...]
    ppermute x21, starting transfers between devices: 48.7 us -> 40.9 us  [send(): return lax.ppermute(x, AXES, moves(fn))]
    concatenate x2 -> x0, other arithmetic: 1.86 us -> none  [the longest x1 1.07 us: on_device(): jnp.concatenate([query_states, jnp.broadcast_to(jnp.tile(ids, HQ)[None, :...]
    ppermute x21, waiting for transfers between devices: 24.5 us -> 25.8 us  [send(): return lax.ppermute(x, AXES, moves(fn))]
  transfers between devices with their start and end apart: 21 -> 21, of which waited for: 11 -> 11; matrix products, arithmetic and copies ran while one was open for 2% -> 3% of each run, Pallas kernels for 0% -> 0%
where the time goes in v2:
time: 101 us; the launch traced here: 102 us
  starting transfers between devices  40.9 us (40%)
  Pallas kernels  29.4 us (29%)
  waiting for transfers between devices  25.8 us (26%)
  local copies, waits for them, and re-layouts  3.1 us (3%)
  other arithmetic  1.91 us (2%)
    ppermute x21, starting transfers between devices, send(): return lax.ppermute(x, AXES, moves(fn))  40.9 us
    pallas_call x3, Pallas kernels, run(): pl.pallas_call(body, out_shape=outs, in_specs=[smem] + [vmem] * len(args)...  29.4 us
    ppermute x21, waiting for transfers between devices, send(): return lax.ppermute(x, AXES, moves(fn))  25.8 us
  transfers between devices with their start and end apart: 21, of which 11 were waited for; matrix products, arithmetic and copies ran while one was open for 3% of the time, Pallas kernels for 0%

profile of v2, /device:TPU:1, one launch (start us, length us, event | category | flops | bytes accessed | tf_op | source)
XLA Modules:
  0.0 101.9 jit_solution(11135659899120662091)
XLA Ops:
  0.6 1.9 %shard_map.76 = (bf16[144,256]{1,0:T(8,128)(2,1)}, bf16[272,1024]{1,0:T(8,128)(2,1)}) custom-call(s32[128]{0:T(128)} %positions.1, bf16[128,1024]{1,0:T(8,128)(2,1)} %q0.3, bf16[128,128]{1,0:T(8,128)(2,1)} %k.1, bf16[128,128]{1,0:T(8,128)(2,1)} %v.1, bf16[128,1024]{1,0:T(8,128)(2,1)} %g0.3), custom_call_target="tpu_custom_call" | custom-call | bytes 6291456 | tf_op jit(solution)/shard_map/pallas_call | solution.py:282
  2.6 3.6 %collective-permute-start.2 = (bf16[272,1024]{1,0:T(8,128)(2,1)}, bf16[272,1024]{1,0:T(8,128)(2,1)S(1)}, u32[]{:S(2)}, u32[]{:S(2)}) collective-permute-start(bf16[272,1024]{1,0:T(8,128)(2,1)} %get-tuple-element.15), channel_id=1, source_target_pairs={{0,24},{4,28},{8,0},{12,4},{16,8},{20,12},{24,16},{28,20},{32,56},... | collective-permute-start | bytes 1671176 | tf_op jit(solution)/shard_map/ppermute | solution.py:49
  6.1 0.0 collective-permute-start.1
  6.1 1.7 %collective-permute-start = (bf16[144,256]{1,0:T(8,128)(2,1)}, bf16[144,256]{1,0:T(8,128)(2,1)S(1)}, u32[]{:S(2)}, u32[]{:S(2)}) collective-permute-start(bf16[144,256]{1,0:T(8,128)(2,1)} %get-tuple-element.14), channel_id=1, source_target_pairs={{0,4},{4,0},{8,12},{12,8},{16,20},{20,16},{24,28},{28,24},{32,36},... | collective-permute-start | bytes 221192 | tf_op jit(solution)/shard_map/ppermute | solution.py:49
  7.8 0.9 constant_dynamic-update-slice_fusion.1
  8.7 0.2 collective-permute-done
  9.0 5.7 %collective-permute-start.4 = (bf16[288,256]{1,0:T(8,128)(2,1)S(1)}, bf16[288,256]{1,0:T(8,128)(2,1)S(1)}, u32[]{:S(2)}, u32[]{:S(2)}) collective-permute-start(bf16[288,256]{1,0:T(8,128)(2,1)S(1)} %constant_dynamic-update-slice_fusion.own), channel_id=1, source_target_pairs={{0,96},{4,164},{8,104},{12,172},{16,112},{20,180},{24,120},{28,188... | collective-permute-start | bytes 442376 | tf_op jit(solution)/shard_map/ppermute | solution.py:49
  14.7 0.7 collective-permute-start.3
  15.4 4.5 %collective-permute-done.4 = bf16[288,256]{1,0:T(8,128)(2,1)S(1)} collective-permute-done((bf16[288,256]{1,0:T(8,128)(2,1)S(1)}, bf16[288,256]{1,0:T(8,128)(2,1)S(1)}, u32[]{:S(2)}, u32[]{:S(2)}) %collective-permute-start.4) | collective-permute-done | bytes 147488 | tf_op jit(solution)/shard_map/ppermute | solution.py:49
  19.9 1.6 %collective-permute-done.3 = bf16[288,256]{1,0:T(8,128)(2,1)S(1)} collective-permute-done((bf16[288,256]{1,0:T(8,128)(2,1)S(1)}, bf16[288,256]{1,0:T(8,128)(2,1)S(1)}, u32[]{:S(2)}, u32[]{:S(2)}) %collective-permute-start.3) | collective-permute-done | bytes 147488 | tf_op jit(solution)/shard_map/ppermute | solution.py:49
  21.5 0.0 collective-permute-done.2.qb
  21.5 0.1 broadcast_select_fusion
  21.6 3.0 %collective-permute-start.6 = (bf16[272,1024]{1,0:T(8,128)(2,1)S(1)}, bf16[272,1024]{1,0:T(8,128)(2,1)S(1)}, u32[]{:S(2)}, u32[]{:S(2)}) collective-permute-start(bf16[272,1024]{1,0:T(8,128)(2,1)S(1)} %broadcast_select_fusion), channel_id=1, source_target_pairs={{0,8},{4,28},{8,16},{12,4},{16,24},{20,12},{24,0},{28,20},{32,40},... | collective-permute-start | bytes 1671176 | tf_op jit(solution)/shard_map/ppermute | solution.py:49
  24.6 3.4 %collective-permute-start.5 = (bf16[432,256]{1,0:T(8,128)(2,1)S(1)}, bf16[432,256]{1,0:T(8,128)(2,1)S(1)}, u32[]{:S(2)}, u32[]{:S(2)}) collective-permute-start(bf16[432,256]{1,0:T(8,128)(2,1)S(1)} %pad_maximum_fusion), channel_id=1, source_target_pairs={{0,32},{4,228},{8,40},{12,236},{16,48},{20,244},{24,56},{28,252},{... | collective-permute-start | bytes 663560 | tf_op jit(solution)/shard_map/ppermute | solution.py:49
  28.0 0.0 copy-start.2
  28.1 0.0 copy-start
  28.1 0.1 collective-permute-start.7
  28.2 2.7 %collective-permute-done.5.kb = bf16[432,256]{1,0:T(8,128)(2,1)S(1)} collective-permute-done((bf16[432,256]{1,0:T(8,128)(2,1)S(1)}, bf16[432,256]{1,0:T(8,128)(2,1)S(1)}, u32[]{:S(2)}, u32[]{:S(2)}) %collective-permute-start.5) | collective-permute-done | bytes 221216 | tf_op jit(solution)/shard_map/ppermute | solution.py:49
  30.9 0.2 collective-permute-done.6.qc
  31.1 2.4 %collective-permute-start.8 = (bf16[432,256]{1,0:T(8,128)(2,1)S(1)}, bf16[432,256]{1,0:T(8,128)(2,1)S(1)}, u32[]{:S(2)}, u32[]{:S(2)}) collective-permute-start(bf16[432,256]{1,0:T(8,128)(2,1)S(1)} %collective-permute-done.5.kb), channel_id=1, source_target_pairs={{0,4},{4,0},{8,12},{12,8},{16,20},{20,16},{24,28},{28,24},{32,36},... | collective-permute-start | bytes 663560 | tf_op jit(solution)/shard_map/ppermute | solution.py:49
  33.5 0.1 slice.84
  33.6 0.1 slice.78
  33.7 0.1 concatenate.47
  33.8 0.1 slice.85
  33.9 0.1 slice.86
  34.0 0.1 slice.79
  34.1 0.1 concatenate.49
  34.2 0.1 slice.82
  34.3 0.1 concatenate.52
  34.4 0.1 slice.87
  34.5 0.1 slice.81
  34.6 0.1 concatenate.51
  34.7 0.1 maximum_convert_fusion
  34.8 0.1 slice.83
  34.9 0.1 concatenate.53
  35.0 0.1 concatenate.54
  35.1 0.2 convert_reduce_fusion
  35.3 0.1 select_reduce_fusion
  35.4 0.2 convert_reduce_fusion.1
  35.6 0.1 concatenate.59.meta
  35.7 10.1 %shard_map.77.st0 = f32[3,8,512]{2,1,0:T(8,128)S(1)} custom-call(s32[96]{0:T(128)S(1)} %concatenate.59.meta, bf16[288,256]{1,0:T(8,128)(2,1)S(1)} %constant_dynamic-update-slice_fusion.own, bf16[576,256]{1,0:T(8,128)(2,1)S(1)} %constant_dynamic-update-slice_fusion.2.ka, bf16[432,256]{1,0:T(8,128)(2,1)S(1)} %collective-permute-done.5.kb, ...), custom_call_target="tpu_custom_call" | custom-call | flops 2147483648 | bytes 6291456 | tf_op jit(solution)/shard_map/pallas_call | solution.py:282
  45.8 0.1 collective-permute-start.11
  45.9 1.4 %collective-permute-start.10 = (f32[3,8,512]{2,1,0:T(8,128)S(1)}, f32[3,8,512]{2,1,0:T(8,128)S(1)}, u32[]{:S(2)}, u32[]{:S(2)}) collective-permute-start(f32[3,8,512]{2,1,0:T(8,128)S(1)} %shard_map.77.st0), channel_id=1, source_target_pairs={{0,24},{4,28},{8,0},{12,4},{16,8},{20,12},{24,16},{28,20},{32,56},... | collective-permute-start | bytes 147464 | tf_op jit(solution)/shard_map/ppermute | solution.py:49
  47.3 0.5 collective-permute-start.9
  47.8 2.6 %collective-permute-done.11.stc = f32[3,8,512]{2,1,0:T(8,128)S(1)} collective-permute-done((f32[3,8,512]{2,1,0:T(8,128)S(1)}, f32[3,8,512]{2,1,0:T(8,128)S(1)}, u32[]{:S(2)}, u32[]{:S(2)}) %collective-permute-start.11) | collective-permute-done | bytes 49184 | tf_op jit(solution)/shard_map/ppermute | solution.py:49
  50.3 1.7 %collective-permute-done.9.sta = f32[3,8,512]{2,1,0:T(8,128)S(1)} collective-permute-done((f32[3,8,512]{2,1,0:T(8,128)S(1)}, f32[3,8,512]{2,1,0:T(8,128)S(1)}, u32[]{:S(2)}, u32[]{:S(2)}) %collective-permute-start.9) | collective-permute-done | bytes 49184 | tf_op jit(solution)/shard_map/ppermute | solution.py:49
  52.0 17.4 %shard_map.78 = (bf16[4,128,1024]{2,1,0:T(8,128)(2,1)S(1)}, bf16[1024,256]{1,0:T(8,128)(2,1)S(1)}, bf16[1024,256]{1,0:T(8,128)(2,1)S(1)}) custom-call(s32[96]{0:T(128)S(1)} %concatenate.59.meta, bf16[288,256]{1,0:T(8,128)(2,1)S(1)} %constant_dynamic-update-slice_fusion.own, bf16[576,256]{1,0:T(8,128)(2,1)S(1)} %constant_dynamic-update-slice_fusion.2.ka, ...), custom_call_target="tpu_custom_call" | custom-call | flops 5368709120 | bytes 6291456 | tf_op jit(solution)/shard_map/pallas_call | solution.py:282
  69.4 4.0 %collective-permute-start.15 = (bf16[1024,256]{1,0:T(8,128)(2,1)S(1)}, bf16[1024,256]{1,0:T(8,128)(2,1)S(1)}, u32[]{:S(2)}, u32[]{:S(2)}) collective-permute-start(bf16[1024,256]{1,0:T(8,128)(2,1)S(1)} %get-tuple-element.24), channel_id=1, source_target_pairs={{0,4},{4,0},{8,12},{12,8},{16,20},{20,16},{24,28},{28,24},{32,36},... | collective-permute-start | bytes 1572872 | tf_op jit(solution)/shard_map/ppermute | solution.py:49
  73.5 1.5 %collective-permute-done.15 = bf16[1024,256]{1,0:T(8,128)(2,1)S(1)} collective-permute-done((bf16[1024,256]{1,0:T(8,128)(2,1)S(1)}, bf16[1024,256]{1,0:T(8,128)(2,1)S(1)}, u32[]{:S(2)}, u32[]{:S(2)}) %collective-permute-start.15) | collective-permute-done | bytes 524320 | tf_op jit(solution)/shard_map/ppermute | solution.py:49
  75.0 0.2 convert_add_fusion
  75.2 1.2 %collective-permute-start.17 = (bf16[256,256]{1,0:T(8,128)(2,1)S(1)}, bf16[256,256]{1,0:T(8,128)(2,1)S(1)}, u32[]{:S(2)}, u32[]{:S(2)}) collective-permute-start(bf16[256,256]{1,0:T(8,128)(2,1)S(1)} %get-tuple-element.34), channel_id=1, source_target_pairs={{0,160},{4,100},{8,168},{12,108},{16,176},{20,116},{24,184},{28,12... | collective-permute-start | bytes 393224 | tf_op jit(solution)/shard_map/ppermute | solution.py:49
  76.4 5.3 %collective-permute-start.19 = (bf16[256,256]{1,0:T(8,128)(2,1)S(1)}, bf16[256,256]{1,0:T(8,128)(2,1)S(1)}, u32[]{:S(2)}, u32[]{:S(2)}) collective-permute-start(bf16[256,256]{1,0:T(8,128)(2,1)S(1)} %get-tuple-element.35), channel_id=1, source_target_pairs={{0,224},{4,36},{8,232},{12,44},{16,240},{20,52},{24,248},{28,60},{... | collective-permute-start | bytes 393224 | tf_op jit(solution)/shard_map/ppermute | solution.py:49
  81.8 3.5 %collective-permute-start.18 = (bf16[256,256]{1,0:T(8,128)(2,1)S(1)}, bf16[256,256]{1,0:T(8,128)(2,1)S(1)}, u32[]{:S(2)}, u32[]{:S(2)}) collective-permute-start(bf16[256,256]{1,0:T(8,128)(2,1)S(1)} %get-tuple-element.36), channel_id=1, source_target_pairs={{0,192},{4,68},{8,200},{12,76},{16,208},{20,84},{24,216},{28,92},{... | collective-permute-start | bytes 393224 | tf_op jit(solution)/shard_map/ppermute | solution.py:49
  85.3 0.1 slice_bitcast_fusion.2
  85.3 0.1 collective-permute-start.12
  85.4 0.1 collective-permute-start.14
  85.5 2.2 %collective-permute-done.17 = bf16[256,256]{1,0:T(8,128)(2,1)S(1)} collective-permute-done((bf16[256,256]{1,0:T(8,128)(2,1)S(1)}, bf16[256,256]{1,0:T(8,128)(2,1)S(1)}, u32[]{:S(2)}, u32[]{:S(2)}) %collective-permute-start.17) | collective-permute-done | bytes 131104 | tf_op jit(solution)/shard_map/ppermute | solution.py:49
  87.8 0.4 collective-permute-start.13
  88.2 3.5 %collective-permute-start.16 = (bf16[128,256]{1,0:T(8,128)(2,1)S(1)}, bf16[128,256]{1,0:T(8,128)(2,1)S(1)}, u32[]{:S(2)}, u32[]{:S(2)}) collective-permute-start(bf16[128,256]{1,0:T(8,128)(2,1)S(1)} %slice.102), channel_id=1, source_target_pairs={{0,128},{4,132},{8,136},{12,140},{16,144},{20,148},{24,152},{28,15... | collective-permute-start | bytes 196616 | tf_op jit(solution)/shard_map/ppermute | solution.py:49
  91.8 0.1 collective-permute-start.20
  91.9 2.9 %collective-permute-done.12 = bf16[128,1024]{1,0:T(8,128)(2,1)S(1)} collective-permute-done((bf16[128,1024]{1,0:T(8,128)(2,1)S(1)}, bf16[128,1024]{1,0:T(8,128)(2,1)S(1)}, u32[]{:S(2)}, u32[]{:S(2)}) %collective-permute-start.12) | collective-permute-done | bytes 262176 | tf_op jit(solution)/shard_map/ppermute | solution.py:49
  94.8 5.6 %collective-permute-done.14 = bf16[128,1024]{1,0:T(8,128)(2,1)S(1)} collective-permute-done((bf16[128,1024]{1,0:T(8,128)(2,1)S(1)}, bf16[128,1024]{1,0:T(8,128)(2,1)S(1)}, u32[]{:S(2)}, u32[]{:S(2)}) %collective-permute-start.14) | collective-permute-done | bytes 262176 | tf_op jit(solution)/shard_map/ppermute | solution.py:49
  100.4 0.9 fusion.2
  101.3 0.6 fusion.8
  (32 shorter events, 0.4 us)
Async XLA Ops:
  2.6 18.9 %collective-permute-start.2 = (bf16[272,1024]{1,0:T(8,128)(2,1)}, bf16[272,1024]{1,0:T(8,128)(2,1)S(1)}, u32[]{:S(2)}, u32[]{:S(2)}) collective-permute-start(bf16[272,1024]{1,0:T(8,128)(2,1)} %get-tuple-element.15), channel_id=1, source_target_pairs={{0,24},{4,28},{8,0},{12,4},{16,8},{20,12},{24,16},{28,20},{32,56},... | collective-permute-start | bytes 1671176 | tf_op jit(solution)/shard_map/ppermute | solution.py:49
  6.1 15.4 %collective-permute-start.1 = (bf16[272,1024]{1,0:T(8,128)(2,1)}, bf16[272,1024]{1,0:T(8,128)(2,1)S(1)}, u32[]{:S(2)}, u32[]{:S(2)}) collective-permute-start(bf16[272,1024]{1,0:T(8,128)(2,1)} %get-tuple-element.15), channel_id=1, source_target_pairs={{0,8},{4,12},{8,16},{12,20},{16,24},{20,28},{24,0},{28,4},{32,40},... | collective-permute-start | bytes 1671176 | tf_op jit(solution)/shard_map/ppermute | solution.py:49
  6.1 2.8 %collective-permute-start = (bf16[144,256]{1,0:T(8,128)(2,1)}, bf16[144,256]{1,0:T(8,128)(2,1)S(1)}, u32[]{:S(2)}, u32[]{:S(2)}) collective-permute-start(bf16[144,256]{1,0:T(8,128)(2,1)} %get-tuple-element.14), channel_id=1, source_target_pairs={{0,4},{4,0},{8,12},{12,8},{16,20},{20,16},{24,28},{28,24},{32,36},... | collective-permute-start | bytes 221192 | tf_op jit(solution)/shard_map/ppermute | solution.py:49
  9.0 11.0 %collective-permute-start.4 = (bf16[288,256]{1,0:T(8,128)(2,1)S(1)}, bf16[288,256]{1,0:T(8,128)(2,1)S(1)}, u32[]{:S(2)}, u32[]{:S(2)}) collective-permute-start(bf16[288,256]{1,0:T(8,128)(2,1)S(1)} %constant_dynamic-update-slice_fusion.own), channel_id=1, source_target_pairs={{0,96},{4,164},{8,104},{12,172},{16,112},{20,180},{24,120},{28,188... | collective-permute-start | bytes 442376 | tf_op jit(solution)/shard_map/ppermute | solution.py:49
  14.7 6.8 %collective-permute-start.3 = (bf16[288,256]{1,0:T(8,128)(2,1)S(1)}, bf16[288,256]{1,0:T(8,128)(2,1)S(1)}, u32[]{:S(2)}, u32[]{:S(2)}) collective-permute-start(bf16[288,256]{1,0:T(8,128)(2,1)S(1)} %constant_dynamic-update-slice_fusion.own), channel_id=1, source_target_pairs={{0,32},{4,228},{8,40},{12,236},{16,48},{20,244},{24,56},{28,252},{... | collective-permute-start | bytes 442376 | tf_op jit(solution)/shard_map/ppermute | solution.py:49
  21.6 9.5 %collective-permute-start.6 = (bf16[272,1024]{1,0:T(8,128)(2,1)S(1)}, bf16[272,1024]{1,0:T(8,128)(2,1)S(1)}, u32[]{:S(2)}, u32[]{:S(2)}) collective-permute-start(bf16[272,1024]{1,0:T(8,128)(2,1)S(1)} %broadcast_select_fusion), channel_id=1, source_target_pairs={{0,8},{4,28},{8,16},{12,4},{16,24},{20,12},{24,0},{28,20},{32,40},... | collective-permute-start | bytes 1671176 | tf_op jit(solution)/shard_map/ppermute | solution.py:49
  24.6 6.3 %collective-permute-start.5 = (bf16[432,256]{1,0:T(8,128)(2,1)S(1)}, bf16[432,256]{1,0:T(8,128)(2,1)S(1)}, u32[]{:S(2)}, u32[]{:S(2)}) collective-permute-start(bf16[432,256]{1,0:T(8,128)(2,1)S(1)} %pad_maximum_fusion), channel_id=1, source_target_pairs={{0,32},{4,228},{8,40},{12,236},{16,48},{20,244},{24,56},{28,252},{... | collective-permute-start | bytes 663560 | tf_op jit(solution)/shard_map/ppermute | solution.py:49
  28.0 7.7 %copy-start.1 = (bf16[128,1024]{1,0:T(8,128)(2,1)S(1)}, bf16[128,1024]{1,0:T(8,128)(2,1)}, u32[]{:S(2)}) copy-start(bf16[128,1024]{1,0:T(8,128)(2,1)} %g0.3) | copy-start | bytes 786436
  28.0 5.4 %copy-start.2 = (s32[128]{0:T(128)S(1)}, s32[128]{0:T(128)}, u32[]{:S(2)}) copy-start(s32[128]{0:T(128)} %positions.1) | copy-start | bytes 1540
  28.1 7.6 %copy-start = (bf16[128,1024]{1,0:T(8,128)(2,1)S(1)}, bf16[128,1024]{1,0:T(8,128)(2,1)}, u32[]{:S(2)}) copy-start(bf16[128,1024]{1,0:T(8,128)(2,1)} %q0.3) | copy-start | bytes 786436
  28.1 6.1 %collective-permute-start.7 = (bf16[576,256]{1,0:T(8,128)(2,1)S(1)}, bf16[576,256]{1,0:T(8,128)(2,1)S(1)}, u32[]{:S(2)}, u32[]{:S(2)}) collective-permute-start(bf16[576,256]{1,0:T(8,128)(2,1)S(1)} %constant_dynamic-update-slice_fusion.2.ka), channel_id=1, source_target_pairs={{0,4},{4,0},{8,12},{12,8},{16,20},{20,16},{24,28},{28,24},{32,36},... | collective-permute-start | bytes 884744 | tf_op jit(solution)/shard_map/ppermute | solution.py:49
  31.1 3.7 %collective-permute-start.8 = (bf16[432,256]{1,0:T(8,128)(2,1)S(1)}, bf16[432,256]{1,0:T(8,128)(2,1)S(1)}, u32[]{:S(2)}, u32[]{:S(2)}) collective-permute-start(bf16[432,256]{1,0:T(8,128)(2,1)S(1)} %collective-permute-done.5.kb), channel_id=1, source_target_pairs={{0,4},{4,0},{8,12},{12,8},{16,20},{20,16},{24,28},{28,24},{32,36},... | collective-permute-start | bytes 663560 | tf_op jit(solution)/shard_map/ppermute | solution.py:49
  45.8 4.5 %collective-permute-start.11 = (f32[3,8,512]{2,1,0:T(8,128)S(1)}, f32[3,8,512]{2,1,0:T(8,128)S(1)}, u32[]{:S(2)}, u32[]{:S(2)}) collective-permute-start(f32[3,8,512]{2,1,0:T(8,128)S(1)} %shard_map.77.st0), channel_id=1, source_target_pairs={{0,16},{4,20},{8,24},{12,28},{16,0},{20,4},{24,8},{28,12},{32,48},... | collective-permute-start | bytes 147464 | tf_op jit(solution)/shard_map/ppermute | solution.py:49
  45.9 4.4 %collective-permute-start.10 = (f32[3,8,512]{2,1,0:T(8,128)S(1)}, f32[3,8,512]{2,1,0:T(8,128)S(1)}, u32[]{:S(2)}, u32[]{:S(2)}) collective-permute-start(f32[3,8,512]{2,1,0:T(8,128)S(1)} %shard_map.77.st0), channel_id=1, source_target_pairs={{0,24},{4,28},{8,0},{12,4},{16,8},{20,12},{24,16},{28,20},{32,56},... | collective-permute-start | bytes 147464 | tf_op jit(solution)/shard_map/ppermute | solution.py:49
  47.3 4.8 %collective-permute-start.9 = (f32[3,8,512]{2,1,0:T(8,128)S(1)}, f32[3,8,512]{2,1,0:T(8,128)S(1)}, u32[]{:S(2)}, u32[]{:S(2)}) collective-permute-start(f32[3,8,512]{2,1,0:T(8,128)S(1)} %shard_map.77.st0), channel_id=1, source_target_pairs={{0,8},{4,12},{8,16},{12,20},{16,24},{20,28},{24,0},{28,4},{32,40},... | collective-permute-start | bytes 147464 | tf_op jit(solution)/shard_map/ppermute | solution.py:49
  69.4 5.6 %collective-permute-start.15 = (bf16[1024,256]{1,0:T(8,128)(2,1)S(1)}, bf16[1024,256]{1,0:T(8,128)(2,1)S(1)}, u32[]{:S(2)}, u32[]{:S(2)}) collective-permute-start(bf16[1024,256]{1,0:T(8,128)(2,1)S(1)} %get-tuple-element.24), channel_id=1, source_target_pairs={{0,4},{4,0},{8,12},{12,8},{16,20},{20,16},{24,28},{28,24},{32,36},... | collective-permute-start | bytes 1572872 | tf_op jit(solution)/shard_map/ppermute | solution.py:49
  75.2 12.6 %collective-permute-start.17 = (bf16[256,256]{1,0:T(8,128)(2,1)S(1)}, bf16[256,256]{1,0:T(8,128)(2,1)S(1)}, u32[]{:S(2)}, u32[]{:S(2)}) collective-permute-start(bf16[256,256]{1,0:T(8,128)(2,1)S(1)} %get-tuple-element.34), channel_id=1, source_target_pairs={{0,160},{4,100},{8,168},{12,108},{16,176},{20,116},{24,184},{28,12... | collective-permute-start | bytes 393224 | tf_op jit(solution)/shard_map/ppermute | solution.py:49
  76.4 11.8 %collective-permute-start.19 = (bf16[256,256]{1,0:T(8,128)(2,1)S(1)}, bf16[256,256]{1,0:T(8,128)(2,1)S(1)}, u32[]{:S(2)}, u32[]{:S(2)}) collective-permute-start(bf16[256,256]{1,0:T(8,128)(2,1)S(1)} %get-tuple-element.35), channel_id=1, source_target_pairs={{0,224},{4,36},{8,232},{12,44},{16,240},{20,52},{24,248},{28,60},{... | collective-permute-start | bytes 393224 | tf_op jit(solution)/shard_map/ppermute | solution.py:49
  81.8 10.0 %collective-permute-start.18 = (bf16[256,256]{1,0:T(8,128)(2,1)S(1)}, bf16[256,256]{1,0:T(8,128)(2,1)S(1)}, u32[]{:S(2)}, u32[]{:S(2)}) collective-permute-start(bf16[256,256]{1,0:T(8,128)(2,1)S(1)} %get-tuple-element.36), channel_id=1, source_target_pairs={{0,192},{4,68},{8,200},{12,76},{16,208},{20,84},{24,216},{28,92},{... | collective-permute-start | bytes 393224 | tf_op jit(solution)/shard_map/ppermute | solution.py:49
  85.3 9.4 %collective-permute-start.12 = (bf16[128,1024]{1,0:T(8,128)(2,1)S(1)}, bf16[128,1024]{1,0:T(8,128)(2,1)S(1)}, u32[]{:S(2)}, u32[]{:S(2)}) collective-permute-start(bf16[128,1024]{1,0:T(8,128)(2,1)S(1)} %get-tuple-element.31), channel_id=1, source_target_pairs={{0,16},{4,20},{8,24},{12,28},{16,0},{20,4},{24,8},{28,12},{32,48},... | collective-permute-start | bytes 786440 | tf_op jit(solution)/shard_map/ppermute | solution.py:49
  85.4 14.9 %collective-permute-start.14 = (bf16[128,1024]{1,0:T(8,128)(2,1)S(1)}, bf16[128,1024]{1,0:T(8,128)(2,1)S(1)}, u32[]{:S(2)}, u32[]{:S(2)}) collective-permute-start(bf16[128,1024]{1,0:T(8,128)(2,1)S(1)} %get-tuple-element.32), channel_id=1, source_target_pairs={{0,8},{4,12},{8,16},{12,20},{16,24},{20,28},{24,0},{28,4},{32,40},... | collective-permute-start | bytes 786440 | tf_op jit(solution)/shard_map/ppermute | solution.py:49
  87.8 12.6 %collective-permute-start.13 = (bf16[128,1024]{1,0:T(8,128)(2,1)S(1)}, bf16[128,1024]{1,0:T(8,128)(2,1)S(1)}, u32[]{:S(2)}, u32[]{:S(2)}) collective-permute-start(bf16[128,1024]{1,0:T(8,128)(2,1)S(1)} %get-tuple-element.33), channel_id=1, source_target_pairs={{0,24},{4,28},{8,0},{12,4},{16,8},{20,12},{24,16},{28,20},{32,56},... | collective-permute-start | bytes 786440 | tf_op jit(solution)/shard_map/ppermute | solution.py:49
  88.2 13.0 %collective-permute-start.16 = (bf16[128,256]{1,0:T(8,128)(2,1)S(1)}, bf16[128,256]{1,0:T(8,128)(2,1)S(1)}, u32[]{:S(2)}, u32[]{:S(2)}) collective-permute-start(bf16[128,256]{1,0:T(8,128)(2,1)S(1)} %slice.102), channel_id=1, source_target_pairs={{0,128},{4,132},{8,136},{12,140},{16,144},{20,148},{24,152},{28,15... | collective-permute-start | bytes 196616 | tf_op jit(solution)/shard_map/ppermute | solution.py:49
  91.8 9.5 %collective-permute-start.20 = (bf16[128,256]{1,0:T(8,128)(2,1)S(1)}, bf16[128,256]{1,0:T(8,128)(2,1)S(1)}, u32[]{:S(2)}, u32[]{:S(2)}) collective-permute-start(bf16[128,256]{1,0:T(8,128)(2,1)S(1)} %slice.123), channel_id=1, source_target_pairs={{0,4},{4,0},{8,12},{12,8},{16,20},{20,16},{24,28},{28,24},{32,36},... | collective-permute-start | bytes 196616 | tf_op jit(solution)/shard_map/ppermute | solution.py:49
